TPU v7x, 256 devices: a whole 4x4x8 slice. The times are simulated.
256 devices in a mesh: dp: 4 (over y), expert: 8 (over z), tensor: 8 (over x, core).
Axes of the slice: x: 4, y: 4, z: 8, core: 2. Of those that a mesh axis runs over, the one named last changes fastest.
Arguments:
- resid: bfloat16 [4, 1024, 3072], P('dp', 'expert'), may hold values from -6 to 6
- queries: bfloat16 [4, 1024, 3072], P('dp', 'expert', 'tensor'), may hold values from -42 to 42
- keys: bfloat16 [4, 1024, 1024], P('dp', 'expert', 'tensor'), may hold values from -7 to 7
- values: bfloat16 [4, 1024, 1024], P('dp', 'expert', 'tensor'), may hold values from -6 to 6
- out_weight: bfloat16 [3072, 3072], P('tensor', ('dp', 'expert')), may hold values from -0.109375 to 0.109375
- norm_gain: float32 [3072], replicated, may hold values from 0.25 to 1.75
- router_weight: bfloat16 [3072, 8], replicated, may hold values from -0.109375 to 0.109375
- gate_weight: bfloat16 [8, 3072, 5376], P('expert', None, 'tensor'), may hold values from -0.109375 to 0.109375
- up_weight: bfloat16 [8, 3072, 5376], P('expert', None, 'tensor'), may hold values from -0.109375 to 0.109375
- down_weight: bfloat16 [8, 5376, 3072], P('expert', 'tensor'), may hold values from -0.078125 to 0.078125
- expert_ids: int32 [4, 1024, 4], P('dp', 'expert'), may hold values from 0 to 7, all different within a row; in each aligned block of 128 rows (0 to 127, 128 to 255, ..., all dimensions but the last counted through in order) at most 80 rows name the same one
Outputs:
- block_out: bfloat16 [4, 1024, 3072], P('dp', ('expert', 'tensor'))
Inputs may be any that keep to these rules, and one draw needn't show every extreme that they name: `expert_ids`: each row names 4 different experts; in every aligned block of 128 rows in order (sequence, position) no expert is named by more than 80 rows, and in some blocks one is named by exactly 80.
All inputs are finite; a program needn't handle non-finite values.
Results may differ from a plain program's by a relative error of at most 0.015.
Values may be sent and summed in bfloat16 or wider, within the bound.
A program may use at most 128 MiB of HBM per device.

v0:
```python
import jax
import jax.numpy as jnp
from jax import lax
from jax.sharding import PartitionSpec as P

HEAD_WIDTH = 128
EXPERTS = 8
TOP = 4
CAP = 80


def expert_part(inputs, gate_weight, up_weight, down_weight, form):
    gate_act = jnp.einsum(
        "sklcd,ldf->sklcf", inputs, gate_weight, preferred_element_type=jnp.float32
    )
    up_act = jnp.einsum("sklcd,ldf->sklcf", inputs, up_weight, preferred_element_type=jnp.float32)
    hidden = (jax.nn.silu(gate_act) * up_act).astype(jnp.bfloat16)
    return jnp.einsum("sklcf,lfd->" + form, hidden, down_weight, preferred_element_type=jnp.float32)


def local(
    resid,
    queries,
    keys,
    values,
    out_weight,
    norm_gain,
    router_weight,
    gate_weight,
    up_weight,
    down_weight,
    expert_ids,
):
    n_tensor = lax.axis_size("tensor")
    n_expert = lax.axis_size("expert")
    block_rows = queries.shape[1]
    heads_local = queries.shape[2] // HEAD_WIDTH
    kv_local = keys.shape[2] // HEAD_WIDTH
    group_size = heads_local // kv_local
    model_width = resid.shape[2]
    whole_keys, whole_values = (
        lax.all_gather(keys, "expert", axis=1, tiled=True),
        lax.all_gather(values, "expert", axis=1, tiled=True),
    )
    seq_len = whole_keys.shape[1]
    query_pos = lax.axis_index("expert") * block_rows + jnp.arange(block_rows, dtype=jnp.int32)
    key_pos = jnp.arange(seq_len, dtype=jnp.int32)
    causal = key_pos[None, :] <= jnp.tile(query_pos, group_size)[:, None]
    query_cube = queries[0].reshape(block_rows, heads_local, HEAD_WIDTH)
    stacked = jnp.transpose(query_cube, (1, 0, 2)).reshape(group_size * block_rows, HEAD_WIDTH)
    single_key = whole_keys[0, :, 0:HEAD_WIDTH]
    value_one = whole_values[0, :, 0:HEAD_WIDTH]
    score_matrix = lax.dot_general(
        stacked, single_key, (((1,), (1,)), ((), ())), preferred_element_type=jnp.float32
    ) * HEAD_WIDTH ** (-0.5)
    score_matrix = jnp.where(causal, score_matrix, -jnp.inf)
    weight_matrix = jax.nn.softmax(score_matrix, axis=-1).astype(jnp.bfloat16)
    mixed_vals = jnp.dot(weight_matrix, value_one, preferred_element_type=jnp.float32).astype(
        jnp.bfloat16
    )
    head_blocks = jnp.transpose(
        mixed_vals.reshape(group_size, block_rows, HEAD_WIDTH), (1, 0, 2)
    ).reshape(block_rows, group_size * HEAD_WIDTH)
    full_out = lax.all_gather(out_weight, ("dp", "expert"), axis=1, tiled=True)
    head_partial = jnp.dot(head_blocks, full_out, preferred_element_type=jnp.float32)
    attention = lax.psum(head_partial.astype(jnp.bfloat16), "tensor").astype(jnp.float32)
    mixed = resid[0].astype(jnp.float32) + attention
    mean_square = jnp.mean(mixed * mixed, axis=-1, keepdims=True)
    normed = (mixed * lax.rsqrt(mean_square + 1e-05) * norm_gain).astype(jnp.bfloat16)
    logits = jnp.dot(normed, router_weight, preferred_element_type=jnp.float32)
    routed = expert_ids[0]
    expert_range = jnp.arange(EXPERTS, dtype=jnp.int32)
    matches = routed[:, :, None] == expert_range[None, None, :]
    gate_scores_topk = jax.nn.sigmoid(jnp.sum(jnp.where(matches, logits[:, None, :], 0.0), axis=-1))
    flat_ids = routed.reshape(-1)
    onehot = (flat_ids[:, None] == expert_range[None, :]).astype(jnp.int32)
    before = jnp.cumsum(onehot, axis=0) - onehot
    slot_index = jnp.sum(before * onehot, axis=1)
    destination = flat_ids * CAP + slot_index
    slot_range = jnp.arange(EXPERTS * CAP, dtype=jnp.int32)
    pair_range = jnp.arange(flat_ids.shape[0], dtype=jnp.int32)
    hits = slot_range[:, None] == destination[None, :]
    source_pair = jnp.sum(jnp.where(hits, pair_range[None, :], 0), axis=1)
    filled = jnp.any(hits, axis=1)
    slot_table = jnp.where(
        filled[:, None], jnp.take(normed, source_pair // TOP, axis=0), jnp.zeros((), jnp.bfloat16)
    )
    local_experts = EXPERTS // n_expert
    share = CAP // n_tensor
    tensor_index = lax.axis_index("tensor")
    table_parts = slot_table.reshape(n_expert, local_experts, n_tensor, share, model_width)
    mine = lax.dynamic_index_in_dim(table_parts, tensor_index, 2, keepdims=False)
    copies = jnp.broadcast_to(
        mine[:, None], (n_expert, n_tensor, local_experts, share, model_width)
    ).reshape(n_expert * n_tensor, local_experts, share, model_width)
    received = lax.all_to_all(copies, ("expert", "tensor"), split_axis=0, concat_axis=0, tiled=True)
    arrived = received.reshape(n_expert, n_tensor, local_experts, share, model_width)
    summed = lax.psum_scatter(
        expert_part(arrived, gate_weight, up_weight, down_weight, "kslcd")
        .reshape(lax.axis_size("tensor") * n_expert, local_experts, share, model_width)
        .astype(jnp.bfloat16),
        "tensor",
        scatter_dimension=0,
        tiled=True,
    )
    returned = lax.all_to_all(summed, "expert", split_axis=0, concat_axis=0, tiled=True)
    gathered = lax.all_gather(returned[:, :, None], "tensor", axis=2, tiled=True)
    expert_rows = gathered.reshape(EXPERTS * CAP, model_width)
    picked = (
        jnp.take(expert_rows, destination, axis=0)
        .reshape(routed.shape[0], TOP, model_width)
        .astype(jnp.float32)
    )
    expert_mix = jnp.sum(gate_scores_topk[:, :, None] * picked, axis=1)
    finished = (mixed + expert_mix).astype(jnp.bfloat16)
    out_rows = block_rows // n_tensor
    return lax.dynamic_slice_in_dim(finished, tensor_index * out_rows, out_rows, 0)[None]


def solution(mesh):
    return jax.shard_map(
        local,
        mesh=mesh,
        in_specs=(
            P("dp", "expert", None),
            P("dp", "expert", "tensor"),
            P("dp", "expert", "tensor"),
            P("dp", "expert", "tensor"),
            P("tensor", ("dp", "expert")),
            P(),
            P(),
            P("expert", None, "tensor"),
            P("expert", None, "tensor"),
            P("expert", "tensor", None),
            P("dp", "expert", None),
        ),
        out_specs=P("dp", ("expert", "tensor"), None),
        check_vma=False,
    )
```

profile of v0, /device:TPU:1, one launch (start us, length us, event | category | flops | bytes accessed | tf_op | source)
XLA Modules:
  0.0 499.7 jit_solution(8873812927773555027)
XLA Ops:
  6.5 0.0 copy-start
  6.5 0.0 all-gather.4.cloned.1.call-start
  6.5 0.7 all-gather.4.cloned.1.call-update
  7.3 0.0 all-reduce.2.cloned.1.call-start
  7.3 0.8 copy.54
  8.1 0.1 reshape_squeeze.7
  8.2 0.1 eq.58
  8.3 1.1 reduce-window.6
  9.5 0.2 slice_reduce_fusion
  9.7 1.0 copy.50
  10.8 0.1 copy.51
  10.9 23.5 %all_gather.12 = bf16[1,1024,128]{2,1,0:T(8,128)(2,1)S(1)} all-gather(bf16[1,128,128]{2,1,0:T(8,128)(2,1)} %param.13), channel_id=1, replica_groups=mesh['dp'=4,'expert'=8,'tensor'=8] {'expert'}, dimensions={1}, use_global_device_ids=true | all-gather | bytes 294912 | tf_op jit(solution)/shard_map/all_gather | solution.py:42
  34.4 19.6 %all_gather.13 = bf16[1,1024,128]{2,1,0:T(8,128)(2,1)S(1)} all-gather(bf16[1,128,128]{2,1,0:T(8,128)(2,1)} %param.14), channel_id=1, replica_groups=mesh['dp'=4,'expert'=8,'tensor'=8] {'expert'}, dimensions={1}, use_global_device_ids=true | all-gather | bytes 294912 | tf_op jit(solution)/shard_map/all_gather | solution.py:43
  54.0 0.5 fusion.39
  54.5 0.4 fusion.24
  54.9 0.4 convolution_convert_fusion.1
  55.3 0.0 copy-start.2
  55.3 0.1 copy.52
  55.5 0.1 fusion.35
  55.6 0.2 select_reduce_fusion
  55.8 0.2 fusion.25
  56.0 32.6 %all-gather.4.cloned.1.call-done = bf16[384,3072]{0,1:T(8,128)(2,1)} async-done(((bf16[384,96]{0,1:T(8,128)(2,1)}), bf16[384,3072]{0,1:T(8,128)(2,1)}) %all-gather.4.cloned.1.call-update) | async-done | bytes 2359312 | tf_op jit(solution)/shard_map/all_gather | solution.py:64
  88.6 3.5 convolution_convert_fusion
  92.1 0.0 all-reduce.2.cloned.1.call-update
  92.1 0.0 reduce-scatter.4.cloned.1.call-start
  92.2 0.1 reduce_sum.68
  92.3 0.2 broadcast_in_dim.95
  92.6 65.2 %all-reduce.2.cloned.1.call-done = bf16[128,3072]{1,0:T(8,128)(2,1)} async-done(((bf16[128,3072]{1,0:T(8,128)(2,1)}), bf16[128,3072]{1,0:T(8,128)(2,1)}) %all-reduce.2.cloned.1.call-update) | async-done | bytes 786448 | tf_op jit(solution)/shard_map/psum | solution.py:66
  157.7 2.6 convert_add_fusion
  160.4 0.3 multiply_convert_fusion
  160.7 4.7 gather_fusion
  165.4 7.3 %gather.13 = bf16[8,1,8,10,3072]{4,3,2,0,1:T(8,128)(2,1)} reshape(bf16[640,3072]{1,0:T(8,128)(2,1)} %gather_fusion) | data formatting | bytes 7864320 | tf_op jit(solution)/shard_map/jit(_take)/gather | solution.py:86
  172.7 1.3 fusion.27
  174.0 0.8 broadcast_in_dim.103
  174.8 0.0 copy-start.6
  174.8 150.3 %all_to_all.10 = bf16[64,1,10,3072]{3,2,1,0:T(8,128)(2,1)S(1)} all-to-all(bf16[64,1,10,3072]{3,2,1,0:T(8,128)(2,1)S(1)} %bitcast.145), channel_id=1, replica_groups=mesh['dp'=4,'expert'=8,'tensor'=8] {'expert','tensor'}, dimensions={0} | all-to-all | bytes 7864320 | tf_op jit(solution)/shard_map/all_to_all | solution.py:96
  325.0 0.0 copy-done.6
  325.1 7.2 %fusion = f32[8,8,10,672]{3,2,1,0:T(8,128)} fusion(bf16[1,3072,672]{1,2,0:T(8,128)(2,1)S(1)} %copy-done.6, bf16[8,8,10,3072]{3,2,1,0:T(8,128)(2,1)S(1)} %bitcast.148), kind=kOutput, calls=%fused_computation.2 | convolution fusion | flops 2642411520 | bytes 9781248 | tf_op jit(solution)/shard_map/sklcd,ldf->sklcf/dot_general | solution.py:16
  332.2 0.0 copy-done.1
  332.2 19.4 %convert_bitcast_fusion = bf16[8,8,1,10,3072]{4,3,0,1,2:T(8,128)(2,1)} fusion(bf16[1,672,3072]{2,1,0:T(8,128)(2,1)} %param.20, f32[8,8,10,672]{3,2,1,0:T(8,128)} %fusion, bf16[1,3072,672]{1,2,0:T(8,128)(2,1)} %param.18, bf16[8,8,10,3072]{3,2,1,0:T(8,128)(2,1)} %bitcast.149), kind=kOutput, calls=%fused_computation.7 | convolution fusion | flops 5289369600 | bytes 17842176 | tf_op jit(solution)/shard_map/sklcf,lfd->kslcd/dot_general | solution.py:18
  351.7 4.9 copy.73
  356.6 2.2 copy.68
  358.8 0.0 reduce-scatter.4.cloned.1.call-update
  358.8 0.0 copy-start.4
  358.8 0.0 all-gather.6.cloned.1.call-start
  358.9 34.9 %reduce-scatter.4.cloned.1.call-done = bf16[8,30720]{1,0:T(8,128)(2,1)} async-done(((bf16[64,30720]{1,0:T(8,128)(2,1)}), bf16[8,30720]{1,0:T(8,128)(2,1)}) %reduce-scatter.4.cloned.1.call-update) | async-done | bytes 491536
  393.8 1.3 copy.59
  395.1 24.8 %all_to_all.11 = bf16[8,1,10,3072]{3,2,1,0:T(8,128)(2,1)S(1)} all-to-all(bf16[8,1,10,3072]{3,2,1,0:T(8,128)(2,1)S(1)} %copy.59), channel_id=1, replica_groups=mesh['dp'=4,'expert'=8,'tensor'=8] {'expert'}, dimensions={0} | all-to-all | bytes 983040 | tf_op jit(solution)/shard_map/all_to_all | solution.py:106
  419.9 1.1 copy.60
  421.0 0.0 all-gather.6.cloned.1.call-update
  421.0 0.1 reduce_sum.66
  421.1 0.1 copy.62
  421.3 0.1 mul.98
  421.4 0.1 copy.56
  421.5 0.1 copy.57
  421.6 0.3 fusion.41
  422.0 0.1 copy.53
  422.1 34.7 %all-gather.6.cloned.1.call-done = bf16[8,8,10,3072]{3,0,2,1:T(8,128)(2,1)} async-done(((bf16[8,1,10,3072]{3,0,2,1:T(8,128)(2,1)}), bf16[8,8,10,3072]{3,0,2,1:T(8,128)(2,1)}) %all-gather.6.cloned.1.call-update) | async-done | bytes 3932176 | tf_op jit(solution)/shard_map/all_gather | solution.py:107
  456.8 7.2 %copy.61 = bf16[8,8,10,3072]{3,2,1,0:T(8,128)(2,1)} copy(bf16[8,8,10,3072]{3,0,2,1:T(8,128)(2,1)} %all-gather.6.cloned.1.call-done) | data formatting | bytes 7864320 | tf_op jit(solution)/shard_map/all_gather | solution.py:107
  463.9 7.5 %reshape.250 = bf16[640,3072]{1,0:T(8,128)(2,1)} reshape(bf16[8,8,10,3072]{3,2,1,0:T(8,128)(2,1)} %copy.61) | data formatting | bytes 7864320 | tf_op jit(solution)/shard_map/reshape | solution.py:108
  471.5 8.7 %gather_fusion.1 = bf16[512,3072]{1,0:T(8,128)(2,1)S(1)} fusion(bf16[640,3072]{1,0:T(8,128)(2,1)} %reshape.250, s32[1024]{0:T(1024)S(1)} %pad_clamp_fusion), kind=kCustom, calls=%fused_computation.1 | custom fusion | bytes 6293504 | tf_op jit(solution)/shard_map/jit(_take)/gather | solution.py:110
  480.2 2.7 gather.15
  482.9 8.7 %multiply_reduce_fusion = f32[128,3072]{1,0:T(8,128)S(1)} fusion(bf16[128,4,3072]{2,1,0:T(4,128)(2,1)} %gather.15, f32[128,4]{1,0:T(8,128)S(1)} %copy.53, pred[128,4]{1,0:T(8,128)(4,1)S(1)} %copy.57), kind=kLoop, calls=%fused_computation.6 | loop fusion | flops 5898240 | bytes 4721152 | tf_op jit(solution)/shard_map/reduce_sum | solution.py:114
  491.6 1.6 fusion.31
  (25 shorter events, 0.3 us)
Async XLA Ops:
  6.5 415.1 %copy-start = (bf16[3072,8]{0,1:T(8,128)(2,1)S(1)}, bf16[3072,8]{0,1:T(8,128)(2,1)}, u32[]{:S(2)}) copy-start(bf16[3072,8]{0,1:T(8,128)(2,1)} %param.17) | copy-start | bytes 147460
  6.5 82.1 %all-gather.4.cloned.1.call-start = ((), (), s32[]{:S(2)}) async-start(), calls=%async_computation.3 | async-start | bytes 2433024 | tf_op jit(solution)/shard_map/all_gather | solution.py:64
  7.3 150.5 %all-reduce.2.cloned.1.call-start = ((), (), s32[]{:S(2)}) async-start(), calls=%async_computation.4 | async-start | bytes 1572864 | tf_op jit(solution)/shard_map/psum | solution.py:66
  55.3 102.4 %copy-start.2 = (bf16[1,128,3072]{2,1,0:T(8,128)(2,1)S(1)}, bf16[1,128,3072]{2,1,0:T(8,128)(2,1)}, u32[]{:S(2)}) copy-start(bf16[1,128,3072]{2,1,0:T(8,128)(2,1)} %param.11) | copy-start | bytes 2359300
  88.6 71.7 %copy-start.5 = (f32[3072]{0:T(1024)S(1)}, f32[3072]{0:T(1024)}, u32[]{:S(2)}) copy-start(f32[3072]{0:T(1024)} %param.16) | copy-start | bytes 36868
  92.1 301.7 %reduce-scatter.4.cloned.1.call-start = ((), (), s32[]{:S(2)}) async-start(), calls=%async_computation.6 | async-start | bytes 4423680
  157.7 2.6 copy-start.3
  174.8 150.3 %copy-start.6 = (bf16[1,3072,672]{1,2,0:T(8,128)(2,1)S(1)}, bf16[1,3072,672]{1,2,0:T(8,128)(2,1)}, u32[]{:S(2)}) copy-start(bf16[1,3072,672]{1,2,0:T(8,128)(2,1)} %param.19) | copy-start | bytes 12386308
  325.0 7.2 %copy-start.1 = (bf16[64,1,10,3072]{3,2,1,0:T(8,128)(2,1)}, bf16[64,1,10,3072]{3,2,1,0:T(8,128)(2,1)S(1)}, u32[]{:S(2)}) copy-start(bf16[64,1,10,3072]{3,2,1,0:T(8,128)(2,1)S(1)} %all_to_all.10) | copy-start | bytes 11796484
  358.8 62.3 %copy-start.4 = (s32[1,128,4]{1,2,0:T(4,128)S(1)}, s32[1,128,4]{1,2,0:T(4,128)}, u32[]{:S(2)}) copy-start(s32[1,128,4]{1,2,0:T(4,128)} %param.21) | copy-start | bytes 6148
  358.8 97.9 %all-gather.6.cloned.1.call-start = ((), (), s32[]{:S(2)}) async-start(), calls=%async_computation.5 | async-start | bytes 4423680 | tf_op jit(solution)/shard_map/all_gather | solution.py:107
Sparse Core Ops, SparseCore 0:
  9.9 78.6 all-gather.3
  92.3 65.4 all-reduce.1
  358.9 34.7 reduce-scatter.3
  421.1 35.5 all-gather.5
where the time goes:
time: 501 us; the launch traced here: 500 us
  blocking collectives  218 us (44%)
  waiting for transfers between devices  168 us (34%)
  local copies, waits for them, and re-layouts  51.8 us (10%)
  matrix products  31.3 us (6%)
  other arithmetic  16.8 us (3%)
  between operations  13.4 us (3%)
    all_to_all x1, blocking collectives, local(): lax.all_to_all(copies, ('expert', 'tensor'), split_axis=0, concat_axis=0,...  150 us
    psum x1, waiting for transfers between devices, local(): lax.psum(head_partial.astype(jnp.bfloat16), 'tensor').astype(jnp.float32)  65.2 us
    unnamed x5, waiting for transfers between devices  35.7 us
    all_gather x1, waiting for transfers between devices, local(): lax.all_gather(returned[:, :, None], 'tensor', axis=2, tiled=True)  34.7 us
    all_gather x1, waiting for transfers between devices, local(): full_out = lax.all_gather(out_weight, ('dp', 'expert'), axis=1, tiled=True)  32.6 us
    all_to_all x1, blocking collectives, local(): lax.all_to_all(summed, 'expert', split_axis=0, concat_axis=0, tiled=True)  24.8 us
    all_gather x1, blocking collectives, local(): lax.all_gather(keys, 'expert', axis=1, tiled=True)  23.5 us
    all_gather x1, blocking collectives, local(): lax.all_gather(values, 'expert', axis=1, tiled=True)  19.6 us
  transfers between devices with their start and end apart: 4, of which 4 were waited for; matrix products, arithmetic and copies ran while one was open for 1% of the time, Pallas kernels for 0%

commit v1 on v0

v1 whole, which is shorter than its diff:
```python
import functools

import jax
import jax.numpy as jnp
from jax import lax
from jax.experimental import pallas as pl
from jax.experimental.pallas import tpu as pltpu
from jax.sharding import PartitionSpec as P

HEAD_WIDTH = 128
CAP = 80
MESH = pl.DeviceIdType.MESH
F32 = jnp.float32
BF16 = jnp.bfloat16
NT = (((1,), (1,)), ((), ()))


def remote(src, dst, send_sem, recv_sem, device):
    return pltpu.make_async_remote_copy(
        src_ref=src,
        dst_ref=dst,
        send_sem=send_sem,
        recv_sem=recv_sem,
        device_id=device,
        device_id_type=MESH,
    )


def greet(devices):
    barrier = pltpu.get_barrier_semaphore()
    for device in devices:
        pl.semaphore_signal(barrier, inc=1, device_id=device, device_id_type=MESH)
    pl.semaphore_wait(barrier, len(devices))


def attention_kernel(
    n_y, n_z, n_t,
    q_ref, k_ref, v_ref, w_ref, resid_ref, gain_ref, router_ref,
    mixed_ref, cols_ref, logit_ref,
    kv, w, scores, heads, part, peer, sums, cross, att, attn, res, sendn,
    kv_ss, kv_rs, w_ss, w_rs, h_ss, h_rs, p_ss, p_rs, x_ss, x_rs, y_ss, y_rs,
    n_ss, n_rs, l_ss, l_rs, res_sem,
):
    n_x = n_t // 2
    y, z, t = lax.axis_index("dp"), lax.axis_index("expert"), lax.axis_index("tensor")
    x, c = lax.div(t, 2), lax.rem(t, 2)
    right, left = lax.rem(z + 1, n_z), lax.rem(z + n_z - 1, n_z)
    rows = q_ref.shape[0]
    group = q_ref.shape[1] // HEAD_WIDTH
    width = mixed_ref.shape[1]
    ycols, tcols, trows = width // n_y, width // n_t, rows // n_t
    per = n_t // n_y
    half = w_ref.shape[0] // 2

    res_copy = pltpu.make_async_copy(
        resid_ref.at[pl.ds(pl.multiple_of(t * trows, trows), trows)], res, res_sem
    )
    res_copy.start()
    kv[z, 0] = k_ref[...]
    kv[z, 1] = v_ref[...]
    w[z] = w_ref[...]
    greet(
        [{"expert": right}, {"expert": left}]
        + [{"dp": lax.rem(y + d, n_y)} for d in range(1, n_y)]
        + [{"tensor": lax.rem(t + d, n_t)} for d in range(1, n_t)]
    )

    hops = n_z // 2

    def kv_hop(way, s):
        block = lax.rem(z + (n_z - s if way == 0 else s), n_z)
        ref = kv.at[block, way] if s == hops - 1 else kv.at[block]
        return remote(
            ref, ref, kv_ss.at[way, s], kv_rs.at[way, s], {"expert": right if way == 0 else left}
        )

    def w_hop(way, s):
        block = lax.rem(z + (n_z - s if way == 0 else s), n_z)
        ref = w.at[block, pl.ds(way * half, half)] if s == hops - 1 else w.at[block]
        return remote(
            ref, ref, w_ss.at[way, s], w_rs.at[way, s], {"expert": right if way == 0 else left}
        )

    def score(block):
        for h in range(group):
            scores[block, h] = lax.dot_general(
                q_ref[:, h * HEAD_WIDTH : (h + 1) * HEAD_WIDTH],
                kv[block, 0],
                NT,
                preferred_element_type=F32,
            )

    for s in range(hops):
        for way in range(2):
            if s > 0:
                kv_hop(way, s - 1).wait_recv()
            kv_hop(way, s).start()
        for way in range(2):
            if s > 0:
                w_hop(way, s - 1).wait_recv()
            w_hop(way, s).start()
        score(lax.rem(z + n_z - s, n_z))
        if s > 0:
            score(lax.rem(z + s, n_z))
    for way in range(2):
        kv_hop(way, hops - 1).wait_recv()
    score(lax.rem(z + hops, n_z))

    all_values = kv[:, 1].reshape(n_z * rows, HEAD_WIDTH)
    shape = (rows, n_z * rows)
    causal = lax.broadcasted_iota(jnp.int32, shape, 1) <= (
        lax.broadcasted_iota(jnp.int32, shape, 0) + z * rows
    )
    for h in range(group):
        s_h = jnp.concatenate([scores[b, h] for b in range(n_z)], axis=1) * HEAD_WIDTH ** (-0.5)
        s_h = jnp.where(causal, s_h, -jnp.inf)
        e_h = jnp.exp(s_h - jnp.max(s_h, axis=1, keepdims=True))
        a_h = (e_h * (1.0 / jnp.sum(e_h, axis=1, keepdims=True))).astype(BF16)
        o_h = jnp.dot(a_h, all_values, preferred_element_type=F32)
        heads[y, :, h * HEAD_WIDTH : (h + 1) * HEAD_WIDTH] = o_h.astype(BF16)

    def heads_copy(d):
        return remote(
            heads.at[y], heads.at[y], h_ss.at[d - 1], h_rs.at[d - 1], {"dp": lax.rem(y + d, n_y)}
        )

    for d in range(1, n_y):
        heads_copy(d).start()
    for way in range(2):
        w_hop(way, hops - 1).wait_recv()

    sibling = {"tensor": t + 1 - 2 * c}
    w_all = w[...].reshape(ycols, w.shape[2])

    def pair_copy(j):
        g = lax.rem(y + n_y - j, n_y)
        return remote(part.at[1 - c, g], peer.at[g], p_ss.at[j], p_rs.at[j], sibling)

    for j in range(n_y):
        g = lax.rem(y + n_y - j, n_y)
        if j > 0:
            heads_copy(j).wait_recv()
        pr = lax.dot_general(heads[g], w_all, NT, preferred_element_type=F32)
        pr = pr.astype(BF16).reshape(n_x, 2, trows, ycols)
        part[0, g] = pr[:, 0]
        part[1, g] = pr[:, 1]
        pair_copy(j).start()
    for j in range(n_y):
        g = lax.rem(y + n_y - j, n_y)
        pair_copy(j).wait_recv()
        sums[:, g] = (part[c, g].astype(F32) + peer[g].astype(F32)).astype(BF16)

    def cross_copy(d):
        to = lax.rem(x + d, n_x)
        return remote(
            sums.at[to], cross.at[d - 1], x_ss.at[d - 1], x_rs.at[d - 1], {"tensor": to * 2 + c}
        )

    for d in range(1, n_x):
        cross_copy(d).start()
    total = sums[x].astype(F32)
    for d in range(1, n_x):
        cross_copy(d).wait_recv()
        total = total + cross[d - 1].astype(F32)
    att[...] = total.astype(BF16)

    def back_copy(d):
        to = lax.rem(y + d, n_y)
        return remote(att.at[to], attn.at[y], y_ss.at[d - 1], y_rs.at[d - 1], {"dp": to})

    for d in range(1, n_y):
        back_copy(d).start()
    attn[y] = att[y]
    res_copy.wait()
    for d in range(1, n_y):
        back_copy(d).wait_recv()

    mixed = []
    square = jnp.zeros((trows, 1), F32)
    for g in range(n_y):
        m_g = res[:, g * ycols : (g + 1) * ycols].astype(F32) + attn[g].astype(F32)
        mixed_ref[:, g * ycols : (g + 1) * ycols] = m_g
        square = square + jnp.sum(m_g * m_g, axis=1, keepdims=True)
        mixed.append(m_g)
    scale = lax.rsqrt(square * (1.0 / width) + 1e-05)
    logits = None
    for g in range(n_y):
        normed = (mixed[g] * scale * gain_ref[:, g * ycols : (g + 1) * ycols]).astype(BF16)
        for i in range(per):
            sendn[g * per + i] = normed[:, i * tcols : (i + 1) * tcols]
        term = lax.dot_general(
            normed,
            router_ref[:, g * ycols : (g + 1) * ycols],
            NT,
            preferred_element_type=F32,
        )
        logits = term if logits is None else logits + term
    lane = lax.broadcasted_iota(jnp.int32, (trows, 128), 1)
    wide = jnp.zeros((trows, 128), F32)
    for e in range(router_ref.shape[0]):
        wide = jnp.where(lane == e, logits[:, e : e + 1], wide)
    logit_ref[t] = wide
    cols_ref[t] = sendn[t]

    def cols_copy(d):
        to = lax.rem(t + d, n_t)
        return remote(
            sendn.at[to], cols_ref.at[t], n_ss.at[d - 1], n_rs.at[d - 1], {"tensor": to}
        )

    def logit_copy(d):
        to = lax.rem(t + d, n_t)
        return remote(
            logit_ref.at[t], logit_ref.at[t], l_ss.at[d - 1], l_rs.at[d - 1], {"tensor": to}
        )

    for d in range(1, n_t):
        cols_copy(d).start()
        logit_copy(d).start()
    for d in range(1, n_t):
        cols_copy(d).wait_recv()
        logit_copy(d).wait_recv()

    for way in range(2):
        for s in range(hops):
            kv_hop(way, s).wait_send()
            w_hop(way, s).wait_send()
    for d in range(1, n_y):
        heads_copy(d).wait_send()
        back_copy(d).wait_send()
    for j in range(n_y):
        pair_copy(j).wait_send()
    for d in range(1, n_x):
        cross_copy(d).wait_send()
    for d in range(1, n_t):
        cols_copy(d).wait_send()
        logit_copy(d).wait_send()


def expert_kernel(
    n_y, n_z, n_t, order,
    cols_ref, logit_ref, ids_ref, mixed_ref, wg_ref, wu_ref, wd_ref,
    out_ref,
    wg, wu, wd, slots, xbuf, table, hidden, act_g, act_u, part, peer, cross, ybuf, zbuf, comb_hi,
    comb_lo, mix, fin,
    wsem, s_ss, s_rs, a_ss, a_rs, b_ss, b_rs, p_ss, p_rs, x_ss, x_rs, z_ss, z_rs, f_ss, f_rs,
):
    n_x = n_t // 2
    y, z, t = lax.axis_index("dp"), lax.axis_index("expert"), lax.axis_index("tensor")
    x, c = lax.div(t, 2), lax.rem(t, 2)
    rows = ids_ref.shape[1]
    width = mixed_ref.shape[1]
    tcols, trows = width // n_t, rows // n_t
    xcols = width // n_x
    halves = 2
    per_half = n_z // halves
    n_groups = 4 if n_z % 4 == 0 else 2
    per_group = n_z // n_groups
    groups_half = n_groups // halves
    hrows, grows = per_half * CAP, per_group * CAP
    sibling_t = t + 1 - 2 * c

    loads = []
    for i in range(n_x):
        span = pl.ds(i * xcols, xcols)
        loads.append(pltpu.make_async_copy(wg_ref.at[:, span], wg.at[i], wsem.at[0, i]))
        loads.append(pltpu.make_async_copy(wu_ref.at[:, span], wu.at[i], wsem.at[1, i]))
    for i in range(n_x):
        span = pl.ds(i * xcols, xcols)
        loads.append(pltpu.make_async_copy(wd_ref.at[:, span], wd.at[i], wsem.at[2, i]))
    for load in loads:
        load.start()
    greet(
        [{"expert": lax.rem(z + d, n_z)} for d in range(1, n_z)]
        + [{"tensor": lax.rem(t + d, n_t)} for d in range(1, n_t)]
    )

    ids = ids_ref[...]
    n_e = table.shape[0]
    expert = lax.broadcasted_iota(jnp.int32, (n_e, rows), 0)
    named = ids[0:1, :] == expert
    for j in range(1, ids.shape[0]):
        named = jnp.logical_or(named, ids[j : j + 1, :] == expert)
    earlier = (
        lax.broadcasted_iota(jnp.int32, (rows, rows), 0)
        < lax.broadcasted_iota(jnp.int32, (rows, rows), 1)
    )
    before = jnp.dot(
        jnp.where(named, 1.0, 0.0).astype(BF16),
        jnp.where(earlier, 1.0, 0.0).astype(BF16),
        preferred_element_type=F32,
    )
    table[...] = jnp.where(named, before.astype(jnp.int32), -1)
    slot = lax.broadcasted_iota(jnp.int32, (CAP, rows), 0)
    cols = cols_ref[...].reshape(rows, tcols)

    def slot_copy(p):
        to = lax.rem(z + n_z - order[p], n_z)
        return remote(
            slots.at[p],
            xbuf.at[t, pl.ds(p * CAP, CAP)],
            s_ss.at[p],
            s_rs.at[p],
            {"expert": to},
        )

    for p in range(n_z):
        e = lax.rem(z + n_z - order[p], n_z)
        pick = jnp.where(table[pl.ds(e, 1), :] == slot, 1.0, 0.0).astype(BF16)
        picked = jnp.dot(pick, cols, preferred_element_type=F32).astype(BF16)
        if p == 0:
            xbuf[t, 0:CAP] = picked
        else:
            slots[p] = picked
            slot_copy(p).start()

    def share_copy(g, d):
        ref = xbuf.at[t, pl.ds(g * grows, grows)]
        to = lax.rem(x + d, n_x) * 2 + c
        return remote(ref, ref, a_ss.at[g, d - 1], a_rs.at[g, d - 1], {"tensor": to})

    def pass_copy(g, d):
        held = lax.rem(x + n_x - d, n_x) * 2 + c
        ref = xbuf.at[held, pl.ds(g * grows, grows)]
        return remote(ref, ref, b_ss.at[g, d], b_rs.at[g, d], {"tensor": sibling_t})

    def share(g):
        for p in range(g * per_group, (g + 1) * per_group):
            if p > 0:
                slot_copy(p).wait_recv()
        for d in range(1, n_x):
            share_copy(g, d).start()
        pass_copy(g, 0).start()

    def forward(g, d):
        share_copy(g, d).wait_recv()
        pass_copy(g, d).start()

    def arrive(g, d):
        pass_copy(g, d).wait_recv()

    def gate_up(h, d):
        i = lax.rem(x + n_x - d, n_x)
        span = pl.ds(h * hrows, hrows)
        held = jnp.concatenate([xbuf[i * 2, span], xbuf[i * 2 + 1, span]], axis=1)
        g_term = lax.dot_general(held, wg[i], NT, preferred_element_type=F32)
        act_g[...] = g_term if d == 0 else act_g[...] + g_term
        u_term = lax.dot_general(held, wu[i], NT, preferred_element_type=F32)
        act_u[...] = u_term if d == 0 else act_u[...] + u_term

    def pair_copy(h, d):
        i = lax.rem(x + d, n_x)
        return remote(
            part.at[h, 1 - c, i], peer.at[h, i], p_ss.at[h, d], p_rs.at[h, d],
            {"tensor": sibling_t},
        )

    def down(h):
        g_all = act_g[...]
        hidden[...] = (g_all / (1.0 + jnp.exp(-g_all)) * act_u[...]).astype(BF16)
        for d in list(range(1, n_x)) + [0]:
            i = lax.rem(x + d, n_x)
            o = jnp.dot(hidden[...], wd[i], preferred_element_type=F32).astype(BF16)
            part[h, 0, i] = o[:, :tcols]
            part[h, 1, i] = o[:, tcols:]
            pair_copy(h, d).start()

    def cross_copy(h, d):
        to = lax.rem(x + d, n_x)
        return remote(
            part.at[h, c, to], cross.at[h, d - 1], x_ss.at[h, d - 1], x_rs.at[h, d - 1],
            {"tensor": to * 2 + c},
        )

    def reduce_send(h):
        for d in list(range(1, n_x)) + [0]:
            i = lax.rem(x + d, n_x)
            pair_copy(h, d).wait_recv()
            part[h, c, i] = (part[h, c, i].astype(F32) + peer[h, i].astype(F32)).astype(BF16)
            if d > 0:
                cross_copy(h, d).start()

    def return_copy(p):
        to = lax.rem(z + order[p], n_z)
        return remote(
            ybuf.at[p], zbuf.at[pl.ds(p * CAP, CAP)], z_ss.at[p], z_rs.at[p], {"expert": to}
        )

    def reduce_recv(h):
        total = part[h, c, x].astype(F32)
        for d in range(1, n_x):
            cross_copy(h, d).wait_recv()
            total = total + cross[h, d - 1].astype(F32)
        total = total.astype(BF16)
        for i in range(per_half):
            p = h * per_half + i
            block = total[i * CAP : (i + 1) * CAP]
            if p == 0:
                zbuf[0:CAP] = block
            else:
                ybuf[p] = block
                return_copy(p).start()

    def of_half(h):
        return range(h * groups_half, (h + 1) * groups_half)

    for g in range(n_groups):
        share(g)
    gates = jnp.transpose(logit_ref[...].reshape(rows, 128))[0:n_e]
    gates = 1.0 / (1.0 + jnp.exp(-gates))
    pieces = []
    for p in range(n_z):
        e = lax.rem(z + n_z - order[p], n_z)
        pick = jnp.where(expert == e, gates, 0.0)
        pick = jnp.sum(pick, axis=0, keepdims=True)
        pieces.append(jnp.where(table[pl.ds(e, 1), :] == slot, pick, 0.0))
    comb = jnp.transpose(jnp.concatenate(pieces, axis=0))
    high = comb.astype(BF16)
    comb_hi[...] = high
    comb_lo[...] = (comb - high.astype(F32)).astype(BF16)
    for load in loads:
        load.wait()
    for h in range(halves):
        for d in list(range(0, n_x)):
            for g in of_half(h):
                if d > 0:
                    forward(g, d)
            for g in of_half(h):
                arrive(g, d)
            gate_up(h, d)
        down(h)
        reduce_send(h)
    for h in range(halves):
        reduce_recv(h)
    for p in range(1, n_z):
        return_copy(p).wait_recv()

    back = zbuf[...]
    mixture = jnp.dot(comb_hi[...], back, preferred_element_type=F32) + jnp.dot(
        comb_lo[...], back, preferred_element_type=F32
    )
    mix[...] = mixture.astype(BF16).reshape(n_t, trows, tcols)

    def final_copy(d):
        to = lax.rem(t + d, n_t)
        return remote(mix.at[to], fin.at[t], f_ss.at[d - 1], f_rs.at[d - 1], {"tensor": to})

    for d in range(1, n_t):
        final_copy(d).start()
    fin[t] = mix[t]
    for d in range(1, n_t):
        final_copy(d).wait_recv()
    for i in range(n_t):
        span = slice(i * tcols, (i + 1) * tcols)
        out_ref[:, span] = (mixed_ref[:, span] + fin[i].astype(F32)).astype(BF16)

    for p in range(1, n_z):
        slot_copy(p).wait_send()
        return_copy(p).wait_send()
    for g in range(n_groups):
        pass_copy(g, 0).wait_send()
        for d in range(1, n_x):
            share_copy(g, d).wait_send()
            pass_copy(g, d).wait_send()
    for h in range(halves):
        for d in range(n_x):
            pair_copy(h, d).wait_send()
            if d > 0:
                cross_copy(h, d).wait_send()
    for d in range(1, n_t):
        final_copy(d).wait_send()


def slot_order(n_z):
    if n_z == 8:
        return (0, 1, 7, 2, 6, 3, 5, 4)
    return tuple(range(n_z))


def local(
    resid, queries, keys, values, out_weight, norm_gain, router_weight,
    gate_weight, up_weight, down_weight, expert_ids,
):
    n_y, n_z, n_t = lax.axis_size("dp"), lax.axis_size("expert"), lax.axis_size("tensor")
    n_x = n_t // 2
    rows, qcols = queries.shape[1], queries.shape[2]
    width = resid.shape[2]
    ff = gate_weight.shape[2]
    n_e = router_weight.shape[1]
    top = expert_ids.shape[2]
    ycols, tcols, trows, xcols = width // n_y, width // n_t, rows // n_t, width // n_x
    wcols = out_weight.shape[1]
    vmem = pl.BlockSpec(memory_space=pltpu.VMEM)
    hbm = pl.BlockSpec(memory_space=pl.ANY)
    dma = pltpu.SemaphoreType.DMA
    V = pltpu.VMEM
    hops = n_z // 2

    mixed, cols, logits = pl.pallas_call(
        functools.partial(attention_kernel, n_y, n_z, n_t),
        out_shape=(
            jax.ShapeDtypeStruct((trows, width), F32),
            jax.ShapeDtypeStruct((n_t, trows, tcols), BF16),
            jax.ShapeDtypeStruct((n_t, trows, 128), F32),
        ),
        in_specs=[vmem, vmem, vmem, vmem, hbm, vmem, vmem],
        out_specs=(vmem, vmem, vmem),
        scratch_shapes=[
            V((n_z, 2, rows, HEAD_WIDTH), BF16),
            V((n_z, wcols, qcols), BF16),
            V((n_z, qcols // HEAD_WIDTH, rows, rows), F32),
            V((n_y, rows, qcols), BF16),
            V((2, n_y, n_x, trows, ycols), BF16),
            V((n_y, n_x, trows, ycols), BF16),
            V((n_x, n_y, trows, ycols), BF16),
            V((n_x - 1, n_y, trows, ycols), BF16),
            V((n_y, trows, ycols), BF16),
            V((n_y, trows, ycols), BF16),
            V((trows, width), BF16),
            V((n_t, trows, tcols), BF16),
            dma((2, hops)), dma((2, hops)), dma((2, hops)), dma((2, hops)),
            dma((n_y - 1,)), dma((n_y - 1,)), dma((n_y,)), dma((n_y,)),
            dma((n_x - 1,)), dma((n_x - 1,)), dma((n_y - 1,)), dma((n_y - 1,)),
            dma((n_t - 1,)), dma((n_t - 1,)), dma((n_t - 1,)), dma((n_t - 1,)),
            dma,
        ],
        compiler_params=pltpu.CompilerParams(
            collective_id=0, has_side_effects=True, vmem_limit_bytes=40 * 2**20
        ),
    )(
        queries[0], keys[0], values[0], out_weight.T, resid[0], norm_gain[None],
        router_weight.T,
    )

    out = pl.pallas_call(
        functools.partial(expert_kernel, n_y, n_z, n_t, slot_order(n_z)),
        out_shape=jax.ShapeDtypeStruct((trows, width), BF16),
        in_specs=[vmem, vmem, vmem, vmem, hbm, hbm, hbm],
        out_specs=vmem,
        scratch_shapes=[
            V((n_x, ff, xcols), BF16),
            V((n_x, ff, xcols), BF16),
            V((n_x, ff, xcols), BF16),
            V((n_z, CAP, tcols), BF16),
            V((n_t, n_z * CAP, tcols), BF16),
            V((n_e, rows), jnp.int32),
            V((n_z // 2 * CAP, ff), BF16),
            V((n_z // 2 * CAP, ff), F32),
            V((n_z // 2 * CAP, ff), F32),
            V((2, 2, n_x, n_z // 2 * CAP, tcols), BF16),
            V((2, n_x, n_z // 2 * CAP, tcols), BF16),
            V((2, n_x - 1, n_z // 2 * CAP, tcols), BF16),
            V((n_z, CAP, tcols), BF16),
            V((n_z * CAP, tcols), BF16),
            V((rows, n_z * CAP), BF16),
            V((rows, n_z * CAP), BF16),
            V((n_t, trows, tcols), BF16),
            V((n_t, trows, tcols), BF16),
            dma((3, n_x)),
            dma((n_z,)), dma((n_z,)),
            dma((4, n_x - 1)), dma((4, n_x - 1)), dma((4, n_x)), dma((4, n_x)),
            dma((2, n_x)), dma((2, n_x)), dma((2, n_x - 1)), dma((2, n_x - 1)),
            dma((n_z,)), dma((n_z,)), dma((n_t - 1,)), dma((n_t - 1,)),
        ],
        compiler_params=pltpu.CompilerParams(
            collective_id=1, has_side_effects=True, vmem_limit_bytes=56 * 2**20
        ),
    )(
        cols, logits, expert_ids[0].T, mixed,
        jnp.swapaxes(gate_weight, 1, 2)[0], jnp.swapaxes(up_weight, 1, 2)[0], down_weight[0],
    )
    return out[None]


def solution(mesh):
    return jax.shard_map(
        local,
        mesh=mesh,
        in_specs=(
            P("dp", "expert", None),
            P("dp", "expert", "tensor"),
            P("dp", "expert", "tensor"),
            P("dp", "expert", "tensor"),
            P("tensor", ("dp", "expert")),
            P(),
            P(),
            P("expert", None, "tensor"),
            P("expert", None, "tensor"),
            P("expert", "tensor", None),
            P("dp", "expert", None),
        ),
        out_specs=P("dp", ("expert", "tensor"), None),
        check_vma=False,
    )
```

time: 501 us -> 131 us (0.26)
  the two profiles are of different devices: /device:TPU:1 before, /device:TPU:33 now
where the time goes in v1:
time: 131 us; the launch traced here: 130 us
  Pallas kernels  121 us (92%)
  local copies, waits for them, and re-layouts  9.4 us (7%)
    pallas_call x1, Pallas kernels, local(): pl.pallas_call(functools.partial(expert_kernel, n_y, n_z, n_t, slot_order...  74.5 us
    pallas_call x1, Pallas kernels, local(): pl.pallas_call(functools.partial(attention_kernel, n_y, n_z, n_t), out_sh...  46.2 us
    unnamed x21, local copies, waits for them, and re-layouts  9.4 us

profile of v1, /device:TPU:33, one launch (start us, length us, event | category | flops | bytes accessed | tf_op | source)
XLA Modules:
  0.0 130.2 jit_solution(5443400784572865700)
XLA Ops:
  0.0 0.0 copy-start
  0.0 1.1 copy-done
  1.1 0.0 copy-start.3
  1.1 0.9 copy-done.3
  2.0 0.0 copy-start.4
  2.0 0.9 copy-done.4
  2.9 0.0 copy-start.6
  2.9 0.8 copy-done.6
  3.7 0.0 copy-start.7
  3.7 0.8 copy-done.7
  4.5 0.0 copy-start.8
  4.5 0.8 copy-done.8
  5.2 0.0 copy-start.9
  5.2 0.7 copy-done.9
  5.9 46.2 %shard_map.109 = (f32[16,3072]{1,0:T(8,128)S(1)}, bf16[8,16,384]{2,1,0:T(8,128)(2,1)S(1)}, f32[8,16,128]{2,1,0:T(8,128)S(1)}) custom-call(bf16[128,384]{1,0:T(8,128)(2,1)S(1)} %bitcast.19, bf16[128,128]{1,0:T(8,128)(2,1)S(1)} %bitcast.22, bf16[128,128]{1,0:T(8,128)(2,1)S(1)} %bitcast.23, bf16[96,384]{1,0:T(8,128)(2,1)S(1)} %bitcast.20, ...), custom_call_target="tpu_custom_call" | custom-call | tf_op jit(solution)/shard_map/pallas_call | solution.py:499
  52.2 0.0 copy-start.1
  52.2 0.7 copy-done.1
  52.9 0.0 copy-start.2
  52.9 0.6 copy-done.2
  53.5 0.0 copy-start.5
  53.5 0.6 copy-done.5
  54.1 74.5 %shard_map.110 = bf16[16,3072]{1,0:T(8,128)(2,1)} custom-call(bf16[8,16,384]{2,1,0:T(8,128)(2,1)} %copy-done.2, f32[8,16,128]{2,1,0:T(8,128)} %copy-done.5, s32[4,128]{1,0:T(4,128)} %bitcast.29, f32[16,3072]{1,0:T(8,128)} %copy-done.1, bf16[672,3072]{1,0:T(8,128)(2,1)} %bitcast.25, bf16[672,3072]{1,0:T(8,128)(2,1)} %bitcast.26, bf16[672,3072]{1,0:T(8,128)(2,1)} %bitcast.27), custom_call_target="tpu_custom_call" | custom-call | tf_op jit(solution)/shard_map/pallas_call | solution.py:535
  128.6 1.5 %copy.13 = bf16[1,16,3072]{2,1,0:T(8,128)(2,1)} copy(bf16[1,16,3072]{2,1,0:T(8,128)(2,1)} %bitcast.28) | data formatting | bytes 196608
Async XLA Ops:
  0.0 1.1 copy-start
  1.1 0.9 copy-start.3
  2.0 0.9 copy-start.4
  2.9 0.8 copy-start.6
  3.7 0.8 copy-start.7
  4.5 0.8 copy-start.8
  5.2 0.7 copy-start.9
  52.2 0.7 copy-start.1
  52.9 0.6 copy-start.2
  53.5 0.6 copy-start.5

commit v2 on v1

--- a/solution.py
+++ b/solution.py
@@ -33,13 +33,18 @@
     pl.semaphore_wait(barrier, len(devices))
 
 
-def attention_kernel(
-    n_y, n_z, n_t,
-    q_ref, k_ref, v_ref, w_ref, resid_ref, gain_ref, router_ref,
-    mixed_ref, cols_ref, logit_ref,
-    kv, w, scores, heads, part, peer, sums, cross, att, attn, res, sendn,
-    kv_ss, kv_rs, w_ss, w_rs, h_ss, h_rs, p_ss, p_rs, x_ss, x_rs, y_ss, y_rs,
-    n_ss, n_rs, l_ss, l_rs, res_sem,
+def block_kernel(
+    n_y, n_z, n_t, order,
+    q_hbm, k_ref, v_ref, w_ref, resid_ref, gain_hbm, router_hbm, ids_hbm, wg_ref, wu_ref, wd_ref,
+    out_ref,
+    q_ref, gain_ref, router_ref, ids_ref, mixed_ref, cols_ref, logit_ref,
+    kv, w, scores, heads, a_part, a_peer, a_sums, a_cross, att, attn, res, sendn,
+    wg, wu, wd, slots, xbuf, table, hidden, act_g, act_u, part, peer, cross, ybuf, zbuf, comb_hi,
+    comb_lo, mix, fin,
+    in_sem, res_sem,
+    kv_ss, kv_rs, w_ss, w_rs, h_ss, h_rs, ap_ss, ap_rs, ax_ss, ax_rs, y_ss, y_rs,
+    n_ss, n_rs, l_ss, l_rs,
+    wsem, s_ss, s_rs, a_ss, a_rs, b_ss, b_rs, p_ss, p_rs, x_ss, x_rs, z_ss, z_rs, f_ss, f_rs,
 ):
     n_x = n_t // 2
     y, z, t = lax.axis_index("dp"), lax.axis_index("expert"), lax.axis_index("tensor")
@@ -48,22 +53,56 @@
     rows = q_ref.shape[0]
     group = q_ref.shape[1] // HEAD_WIDTH
     width = mixed_ref.shape[1]
-    ycols, tcols, trows = width // n_y, width // n_t, rows // n_t
+    ycols, tcols, trows, xcols = width // n_y, width // n_t, rows // n_t, width // n_x
     per = n_t // n_y
     half = w_ref.shape[0] // 2
+    halves = 2
+    per_half = n_z // halves
+    n_groups = 4 if n_z % 4 == 0 else 2
+    per_group = n_z // n_groups
+    groups_half = n_groups // halves
+    hrows, grows = per_half * CAP, per_group * CAP
+    sibling_t = t + 1 - 2 * c
+    sent = []
+
+    def go(copy):
+        copy.start()
+        sent.append(copy)
 
     res_copy = pltpu.make_async_copy(
         resid_ref.at[pl.ds(pl.multiple_of(t * trows, trows), trows)], res, res_sem
     )
-    res_copy.start()
-    kv[z, 0] = k_ref[...]
-    kv[z, 1] = v_ref[...]
-    w[z] = w_ref[...]
+    first = [
+        pltpu.make_async_copy(k_ref, kv.at[z, 0], in_sem.at[0]),
+        pltpu.make_async_copy(v_ref, kv.at[z, 1], in_sem.at[1]),
+        pltpu.make_async_copy(w_ref, w.at[z], in_sem.at[2]),
+        pltpu.make_async_copy(q_hbm, q_ref, in_sem.at[3]),
+    ]
+    later = [
+        pltpu.make_async_copy(gain_hbm, gain_ref, in_sem.at[4]),
+        pltpu.make_async_copy(router_hbm, router_ref, in_sem.at[5]),
+        pltpu.make_async_copy(ids_hbm, ids_ref, in_sem.at[6]),
+        res_copy,
+    ]
+    for copy in first + later:
+        copy.start()
     greet(
-        [{"expert": right}, {"expert": left}]
+        [{"expert": lax.rem(z + d, n_z)} for d in range(1, n_z)]
         + [{"dp": lax.rem(y + d, n_y)} for d in range(1, n_y)]
         + [{"tensor": lax.rem(t + d, n_t)} for d in range(1, n_t)]
     )
+    for copy in first:
+        copy.wait()
+    loads = []
+    for i in range(n_x):
+        span = pl.ds(i * xcols, xcols)
+        loads.append(pltpu.make_async_copy(wg_ref.at[:, span], wg.at[i], wsem.at[0, i]))
+        loads.append(pltpu.make_async_copy(wu_ref.at[:, span], wu.at[i], wsem.at[1, i]))
+    for i in range(n_x):
+        span = pl.ds(i * xcols, xcols)
+        loads.append(pltpu.make_async_copy(wd_ref.at[:, span], wd.at[i], wsem.at[2, i]))
+    for load in loads:
+        load.start()
 
     hops = n_z // 2
 
@@ -94,11 +133,11 @@
         for way in range(2):
             if s > 0:
                 kv_hop(way, s - 1).wait_recv()
-            kv_hop(way, s).start()
+            go(kv_hop(way, s))
         for way in range(2):
             if s > 0:
                 w_hop(way, s - 1).wait_recv()
-            w_hop(way, s).start()
+            go(w_hop(way, s))
         score(lax.rem(z + n_z - s, n_z))
         if s > 0:
             score(lax.rem(z + s, n_z))
@@ -125,16 +164,16 @@
         )
 
     for d in range(1, n_y):
-        heads_copy(d).start()
+        go(heads_copy(d))
     for way in range(2):
         w_hop(way, hops - 1).wait_recv()
 
     sibling = {"tensor": t + 1 - 2 * c}
     w_all = w[...].reshape(ycols, w.shape[2])
 
-    def pair_copy(j):
+    def head_pair(j):
         g = lax.rem(y + n_y - j, n_y)
-        return remote(part.at[1 - c, g], peer.at[g], p_ss.at[j], p_rs.at[j], sibling)
+        return remote(a_part.at[1 - c, g], a_peer.at[g], ap_ss.at[j], ap_rs.at[j], sibling)
 
     for j in range(n_y):
         g = lax.rem(y + n_y - j, n_y)
@@ -142,26 +181,26 @@
             heads_copy(j).wait_recv()
         pr = lax.dot_general(heads[g], w_all, NT, preferred_element_type=F32)
         pr = pr.astype(BF16).reshape(n_x, 2, trows, ycols)
-        part[0, g] = pr[:, 0]
-        part[1, g] = pr[:, 1]
-        pair_copy(j).start()
+        a_part[0, g] = pr[:, 0]
+        a_part[1, g] = pr[:, 1]
+        go(head_pair(j))
     for j in range(n_y):
         g = lax.rem(y + n_y - j, n_y)
-        pair_copy(j).wait_recv()
-        sums[:, g] = (part[c, g].astype(F32) + peer[g].astype(F32)).astype(BF16)
-
-    def cross_copy(d):
+        head_pair(j).wait_recv()
+        a_sums[:, g] = (a_part[c, g].astype(F32) + a_peer[g].astype(F32)).astype(BF16)
+
+    def head_cross(d):
         to = lax.rem(x + d, n_x)
         return remote(
-            sums.at[to], cross.at[d - 1], x_ss.at[d - 1], x_rs.at[d - 1], {"tensor": to * 2 + c}
+            a_sums.at[to], a_cross.at[d - 1], ax_ss.at[d - 1], ax_rs.at[d - 1], {"tensor": to * 2 + c}
         )
 
     for d in range(1, n_x):
-        cross_copy(d).start()
-    total = sums[x].astype(F32)
+        go(head_cross(d))
+    total = a_sums[x].astype(F32)
     for d in range(1, n_x):
-        cross_copy(d).wait_recv()
-        total = total + cross[d - 1].astype(F32)
+        head_cross(d).wait_recv()
+        total = total + a_cross[d - 1].astype(F32)
     att[...] = total.astype(BF16)
 
     def back_copy(d):
@@ -169,9 +208,10 @@
         return remote(att.at[to], attn.at[y], y_ss.at[d - 1], y_rs.at[d - 1], {"dp": to})
 
     for d in range(1, n_y):
-        back_copy(d).start()
+        go(back_copy(d))
     attn[y] = att[y]
-    res_copy.wait()
+    for copy in later:
+        copy.wait()
     for d in range(1, n_y):
         back_copy(d).wait_recv()
 
@@ -215,65 +255,11 @@
         )
 
     for d in range(1, n_t):
-        cols_copy(d).start()
-        logit_copy(d).start()
+        go(cols_copy(d))
+        go(logit_copy(d))
     for d in range(1, n_t):
         cols_copy(d).wait_recv()
         logit_copy(d).wait_recv()
-
-    for way in range(2):
-        for s in range(hops):
-            kv_hop(way, s).wait_send()
-            w_hop(way, s).wait_send()
-    for d in range(1, n_y):
-        heads_copy(d).wait_send()
-        back_copy(d).wait_send()
-    for j in range(n_y):
-        pair_copy(j).wait_send()
-    for d in range(1, n_x):
-        cross_copy(d).wait_send()
-    for d in range(1, n_t):
-        cols_copy(d).wait_send()
-        logit_copy(d).wait_send()
-
-
-def expert_kernel(
-    n_y, n_z, n_t, order,
-    cols_ref, logit_ref, ids_ref, mixed_ref, wg_ref, wu_ref, wd_ref,
-    out_ref,
-    wg, wu, wd, slots, xbuf, table, hidden, act_g, act_u, part, peer, cross, ybuf, zbuf, comb_hi,
-    comb_lo, mix, fin,
-    wsem, s_ss, s_rs, a_ss, a_rs, b_ss, b_rs, p_ss, p_rs, x_ss, x_rs, z_ss, z_rs, f_ss, f_rs,
-):
-    n_x = n_t // 2
-    y, z, t = lax.axis_index("dp"), lax.axis_index("expert"), lax.axis_index("tensor")
-    x, c = lax.div(t, 2), lax.rem(t, 2)
-    rows = ids_ref.shape[1]
-    width = mixed_ref.shape[1]
-    tcols, trows = width // n_t, rows // n_t
-    xcols = width // n_x
-    halves = 2
-    per_half = n_z // halves
-    n_groups = 4 if n_z % 4 == 0 else 2
-    per_group = n_z // n_groups
-    groups_half = n_groups // halves
-    hrows, grows = per_half * CAP, per_group * CAP
-    sibling_t = t + 1 - 2 * c
-
-    loads = []
-    for i in range(n_x):
-        span = pl.ds(i * xcols, xcols)
-        loads.append(pltpu.make_async_copy(wg_ref.at[:, span], wg.at[i], wsem.at[0, i]))
-        loads.append(pltpu.make_async_copy(wu_ref.at[:, span], wu.at[i], wsem.at[1, i]))
-    for i in range(n_x):
-        span = pl.ds(i * xcols, xcols)
-        loads.append(pltpu.make_async_copy(wd_ref.at[:, span], wd.at[i], wsem.at[2, i]))
-    for load in loads:
-        load.start()
-    greet(
-        [{"expert": lax.rem(z + d, n_z)} for d in range(1, n_z)]
-        + [{"tensor": lax.rem(t + d, n_t)} for d in range(1, n_t)]
-    )
 
     ids = ids_ref[...]
     n_e = table.shape[0]
@@ -312,7 +298,7 @@
             xbuf[t, 0:CAP] = picked
         else:
             slots[p] = picked
-            slot_copy(p).start()
+            go(slot_copy(p))
 
     def share_copy(g, d):
         ref = xbuf.at[t, pl.ds(g * grows, grows)]
@@ -329,12 +315,12 @@
             if p > 0:
                 slot_copy(p).wait_recv()
         for d in range(1, n_x):
-            share_copy(g, d).start()
-        pass_copy(g, 0).start()
+            go(share_copy(g, d))
+        go(pass_copy(g, 0))
 
     def forward(g, d):
         share_copy(g, d).wait_recv()
-        pass_copy(g, d).start()
+        go(pass_copy(g, d))
 
     def arrive(g, d):
         pass_copy(g, d).wait_recv()
@@ -363,7 +349,7 @@
             o = jnp.dot(hidden[...], wd[i], preferred_element_type=F32).astype(BF16)
             part[h, 0, i] = o[:, :tcols]
             part[h, 1, i] = o[:, tcols:]
-            pair_copy(h, d).start()
+            go(pair_copy(h, d))
 
     def cross_copy(h, d):
         to = lax.rem(x + d, n_x)
@@ -378,7 +364,7 @@
             pair_copy(h, d).wait_recv()
             part[h, c, i] = (part[h, c, i].astype(F32) + peer[h, i].astype(F32)).astype(BF16)
             if d > 0:
-                cross_copy(h, d).start()
+                go(cross_copy(h, d))
 
     def return_copy(p):
         to = lax.rem(z + order[p], n_z)
@@ -399,7 +385,7 @@
                 zbuf[0:CAP] = block
             else:
                 ybuf[p] = block
-                return_copy(p).start()
+                go(return_copy(p))
 
     def of_half(h):
         return range(h * groups_half, (h + 1) * groups_half)
@@ -446,7 +432,7 @@
         return remote(mix.at[to], fin.at[t], f_ss.at[d - 1], f_rs.at[d - 1], {"tensor": to})
 
     for d in range(1, n_t):
-        final_copy(d).start()
+        go(final_copy(d))
     fin[t] = mix[t]
     for d in range(1, n_t):
         final_copy(d).wait_recv()
@@ -454,21 +440,8 @@
         span = slice(i * tcols, (i + 1) * tcols)
         out_ref[:, span] = (mixed_ref[:, span] + fin[i].astype(F32)).astype(BF16)
 
-    for p in range(1, n_z):
-        slot_copy(p).wait_send()
-        return_copy(p).wait_send()
-    for g in range(n_groups):
-        pass_copy(g, 0).wait_send()
-        for d in range(1, n_x):
-            share_copy(g, d).wait_send()
-            pass_copy(g, d).wait_send()
-    for h in range(halves):
-        for d in range(n_x):
-            pair_copy(h, d).wait_send()
-            if d > 0:
-                cross_copy(h, d).wait_send()
-    for d in range(1, n_t):
-        final_copy(d).wait_send()
+    for copy in sent:
+        copy.wait_send()
 
 
 def slot_order(n_z):
@@ -490,22 +463,25 @@
     top = expert_ids.shape[2]
     ycols, tcols, trows, xcols = width // n_y, width // n_t, rows // n_t, width // n_x
     wcols = out_weight.shape[1]
-    vmem = pl.BlockSpec(memory_space=pltpu.VMEM)
-    hbm = pl.BlockSpec(memory_space=pl.ANY)
+    hrows = n_z // 2 * CAP
+    hbm = pl.BlockSpec(memory_space=pltpu.HBM)
     dma = pltpu.SemaphoreType.DMA
     V = pltpu.VMEM
     hops = n_z // 2
 
-    mixed, cols, logits = pl.pallas_call(
-        functools.partial(attention_kernel, n_y, n_z, n_t),
-        out_shape=(
-            jax.ShapeDtypeStruct((trows, width), F32),
-            jax.ShapeDtypeStruct((n_t, trows, tcols), BF16),
-            jax.ShapeDtypeStruct((n_t, trows, 128), F32),
-        ),
-        in_specs=[vmem, vmem, vmem, vmem, hbm, vmem, vmem],
-        out_specs=(vmem, vmem, vmem),
+    out = pl.pallas_call(
+        functools.partial(block_kernel, n_y, n_z, n_t, slot_order(n_z)),
+        out_shape=jax.ShapeDtypeStruct((trows, width), BF16),
+        in_specs=[hbm] * 11,
+        out_specs=pl.BlockSpec(memory_space=pltpu.VMEM),
         scratch_shapes=[
+            V((rows, qcols), BF16),
+            V((1, width), F32),
+            V((n_e, width), BF16),
+            V((top, rows), jnp.int32),
+            V((trows, width), F32),
+            V((n_t, trows, tcols), BF16),
+            V((n_t, trows, 128), F32),
             V((n_z, 2, rows, HEAD_WIDTH), BF16),
             V((n_z, wcols, qcols), BF16),
             V((n_z, qcols // HEAD_WIDTH, rows, rows), F32),
@@ -518,44 +494,29 @@
             V((n_y, trows, ycols), BF16),
             V((trows, width), BF16),
             V((n_t, trows, tcols), BF16),
-            dma((2, hops)), dma((2, hops)), dma((2, hops)), dma((2, hops)),
-            dma((n_y - 1,)), dma((n_y - 1,)), dma((n_y,)), dma((n_y,)),
-            dma((n_x - 1,)), dma((n_x - 1,)), dma((n_y - 1,)), dma((n_y - 1,)),
-            dma((n_t - 1,)), dma((n_t - 1,)), dma((n_t - 1,)), dma((n_t - 1,)),
-            dma,
-        ],
-        compiler_params=pltpu.CompilerParams(
-            collective_id=0, has_side_effects=True, vmem_limit_bytes=40 * 2**20
-        ),
-    )(
-        queries[0], keys[0], values[0], out_weight.T, resid[0], norm_gain[None],
-        router_weight.T,
-    )
-
-    out = pl.pallas_call(
-        functools.partial(expert_kernel, n_y, n_z, n_t, slot_order(n_z)),
-        out_shape=jax.ShapeDtypeStruct((trows, width), BF16),
-        in_specs=[vmem, vmem, vmem, vmem, hbm, hbm, hbm],
-        out_specs=vmem,
-        scratch_shapes=[
             V((n_x, ff, xcols), BF16),
             V((n_x, ff, xcols), BF16),
             V((n_x, ff, xcols), BF16),
             V((n_z, CAP, tcols), BF16),
             V((n_t, n_z * CAP, tcols), BF16),
             V((n_e, rows), jnp.int32),
-            V((n_z // 2 * CAP, ff), BF16),
-            V((n_z // 2 * CAP, ff), F32),
-            V((n_z // 2 * CAP, ff), F32),
-            V((2, 2, n_x, n_z // 2 * CAP, tcols), BF16),
-            V((2, n_x, n_z // 2 * CAP, tcols), BF16),
-            V((2, n_x - 1, n_z // 2 * CAP, tcols), BF16),
+            V((hrows, ff), BF16),
+            V((hrows, ff), F32),
+            V((hrows, ff), F32),
+            V((2, 2, n_x, hrows, tcols), BF16),
+            V((2, n_x, hrows, tcols), BF16),
+            V((2, n_x - 1, hrows, tcols), BF16),
             V((n_z, CAP, tcols), BF16),
             V((n_z * CAP, tcols), BF16),
             V((rows, n_z * CAP), BF16),
             V((rows, n_z * CAP), BF16),
             V((n_t, trows, tcols), BF16),
             V((n_t, trows, tcols), BF16),
+            dma((7,)), dma,
+            dma((2, hops)), dma((2, hops)), dma((2, hops)), dma((2, hops)),
+            dma((n_y - 1,)), dma((n_y - 1,)), dma((n_y,)), dma((n_y,)),
+            dma((n_x - 1,)), dma((n_x - 1,)), dma((n_y - 1,)), dma((n_y - 1,)),
+            dma((n_t - 1,)), dma((n_t - 1,)), dma((n_t - 1,)), dma((n_t - 1,)),
             dma((3, n_x)),
             dma((n_z,)), dma((n_z,)),
             dma((4, n_x - 1)), dma((4, n_x - 1)), dma((4, n_x)), dma((4, n_x)),
@@ -563,10 +524,11 @@
             dma((n_z,)), dma((n_z,)), dma((n_t - 1,)), dma((n_t - 1,)),
         ],
         compiler_params=pltpu.CompilerParams(
-            collective_id=1, has_side_effects=True, vmem_limit_bytes=56 * 2**20
+            collective_id=0, has_side_effects=True, vmem_limit_bytes=58 * 2**20
         ),
     )(
-        cols, logits, expert_ids[0].T, mixed,
+        queries[0], keys[0], values[0], out_weight.T, resid[0], norm_gain[None],
+        router_weight.T, expert_ids[0].T,
         jnp.swapaxes(gate_weight, 1, 2)[0], jnp.swapaxes(up_weight, 1, 2)[0], down_weight[0],
     )
     return out[None]

time: 131 us -> 118 us (0.901)
  the two profiles are of different devices: /device:TPU:33 before, /device:TPU:1 now
where the time goes in v2:
time: 118 us; the launch traced here: 116 us
  Pallas kernels  115 us (97%)
  local copies, waits for them, and re-layouts  1.54 us (1%)
    pallas_call x1, Pallas kernels, local(): pl.pallas_call(functools.partial(block_kernel, n_y, n_z, n_t, slot_order(...  115 us

profile of v2, /device:TPU:1, one launch (start us, length us, event | category | flops | bytes accessed | tf_op | source)
XLA Modules:
  0.0 116.3 jit_solution(12730349622357459822)
XLA Ops:
  0.0 114.8 %shard_map.109 = bf16[16,3072]{1,0:T(8,128)(2,1)} custom-call(bf16[128,384]{1,0:T(8,128)(2,1)} %bitcast.23, bf16[128,128]{1,0:T(8,128)(2,1)} %bitcast.26, bf16[128,128]{1,0:T(8,128)(2,1)} %bitcast.27, bf16[96,384]{1,0:T(8,128)(2,1)} %bitcast.24, bf16[128,3072]{1,0:T(8,128)(2,1)} %bitcast.21, f32[1,3072]{1,0:T(1,128)} %bitcast.28, bf16[8,3072]{1,0:T(8,128)(2,1)} %bitcast.25, ...), custom_call_target="tpu_custom_call" | custom-call | tf_op jit(solution)/shard_map/pallas_call | solution.py:472
  114.8 1.5 %copy.13 = bf16[1,16,3072]{2,1,0:T(8,128)(2,1)} copy(bf16[1,16,3072]{2,1,0:T(8,128)(2,1)} %bitcast.22) | data formatting | bytes 196608

commit v3 on v2

--- a/solution.py
+++ b/solution.py
@@ -37,14 +37,15 @@
     n_y, n_z, n_t, order,
     q_hbm, k_ref, v_ref, w_ref, resid_ref, gain_hbm, router_hbm, ids_hbm, wg_ref, wu_ref, wd_ref,
     out_ref,
-    q_ref, gain_ref, router_ref, ids_ref, mixed_ref, cols_ref, logit_ref,
+    q_ref, gain_ref, router_ref, ids_all, mixed_ref, zc, logit_ref,
     kv, w, scores, heads, a_part, a_peer, a_sums, a_cross, att, attn, res, sendn,
-    wg, wu, wd, slots, xbuf, table, hidden, act_g, act_u, part, peer, cross, ybuf, zbuf, comb_hi,
-    comb_lo, mix, fin,
+    wg, wu, wd, xbuf, table, mine, hidden, act_g, act_u, part, peer, vbuf, cross, ybuf, zbuf,
+    comb_hi, comb_lo, mix, fin,
     in_sem, res_sem,
     kv_ss, kv_rs, w_ss, w_rs, h_ss, h_rs, ap_ss, ap_rs, ax_ss, ax_rs, y_ss, y_rs,
-    n_ss, n_rs, l_ss, l_rs,
-    wsem, s_ss, s_rs, a_ss, a_rs, b_ss, b_rs, p_ss, p_rs, x_ss, x_rs, z_ss, z_rs, f_ss, f_rs,
+    n_ss, n_rs, l_ss, l_rs, i_ss, i_rs,
+    wsem, s_ss, s_rs, a_ss, a_rs, b_ss, b_rs, p_ss, p_rs, v_ss, v_rs, x_ss, x_rs, z_ss, z_rs,
+    f_ss, f_rs,
 ):
     n_x = n_t // 2
     y, z, t = lax.axis_index("dp"), lax.axis_index("expert"), lax.axis_index("tensor")
@@ -58,10 +59,11 @@
     half = w_ref.shape[0] // 2
     halves = 2
     per_half = n_z // halves
-    n_groups = 4 if n_z % 4 == 0 else 2
-    per_group = n_z // n_groups
-    groups_half = n_groups // halves
-    hrows, grows = per_half * CAP, per_group * CAP
+    n_units = 4 if n_z % 4 == 0 else 2
+    per_unit = n_z // n_units
+    units_half = n_units // halves
+    hrows, urows = per_half * CAP, per_unit * CAP
+    near = (1, n_x - 1) if n_x > 2 else (1,)
     sibling_t = t + 1 - 2 * c
     sent = []
 
@@ -77,11 +79,11 @@
         pltpu.make_async_copy(v_ref, kv.at[z, 1], in_sem.at[1]),
         pltpu.make_async_copy(w_ref, w.at[z], in_sem.at[2]),
         pltpu.make_async_copy(q_hbm, q_ref, in_sem.at[3]),
+        pltpu.make_async_copy(ids_hbm, ids_all.at[z], in_sem.at[6]),
     ]
     later = [
         pltpu.make_async_copy(gain_hbm, gain_ref, in_sem.at[4]),
         pltpu.make_async_copy(router_hbm, router_ref, in_sem.at[5]),
-        pltpu.make_async_copy(ids_hbm, ids_ref, in_sem.at[6]),
         res_copy,
     ]
     for copy in first + later:
@@ -129,21 +131,42 @@
                 preferred_element_type=F32,
             )
 
+    def w_step(s):
+        for way in range(2):
+            if s > 0:
+                w_hop(way, s - 1).wait_recv()
+            if s < hops:
+                go(w_hop(way, s))
+
+    def ids_copy(d):
+        to = lax.rem(z + d, n_z)
+        return remote(
+            ids_all.at[z], ids_all.at[z], i_ss.at[d - 1], i_rs.at[d - 1], {"expert": to}
+        )
+
+    w_done = 0
     for s in range(hops):
         for way in range(2):
             if s > 0:
                 kv_hop(way, s - 1).wait_recv()
             go(kv_hop(way, s))
-        for way in range(2):
-            if s > 0:
-                w_hop(way, s - 1).wait_recv()
-            go(w_hop(way, s))
+        if s % 2 == 1:
+            w_step(w_done)
+            w_done += 1
         score(lax.rem(z + n_z - s, n_z))
         if s > 0:
             score(lax.rem(z + s, n_z))
     for way in range(2):
         kv_hop(way, hops - 1).wait_recv()
     score(lax.rem(z + hops, n_z))
+    for d in range(1, n_z):
+        go(ids_copy(d))
+
+    def heads_copy(d, h):
+        return remote(
+            heads.at[y, h], heads.at[y, h], h_ss.at[d - 1, h], h_rs.at[d - 1, h],
+            {"dp": lax.rem(y + d, n_y)},
+        )
 
     all_values = kv[:, 1].reshape(n_z * rows, HEAD_WIDTH)
     shape = (rows, n_z * rows)
@@ -156,17 +179,15 @@
         e_h = jnp.exp(s_h - jnp.max(s_h, axis=1, keepdims=True))
         a_h = (e_h * (1.0 / jnp.sum(e_h, axis=1, keepdims=True))).astype(BF16)
         o_h = jnp.dot(a_h, all_values, preferred_element_type=F32)
-        heads[y, :, h * HEAD_WIDTH : (h + 1) * HEAD_WIDTH] = o_h.astype(BF16)
-
-    def heads_copy(d):
-        return remote(
-            heads.at[y], heads.at[y], h_ss.at[d - 1], h_rs.at[d - 1], {"dp": lax.rem(y + d, n_y)}
-        )
-
-    for d in range(1, n_y):
-        go(heads_copy(d))
-    for way in range(2):
-        w_hop(way, hops - 1).wait_recv()
+        heads[y, h] = o_h.astype(BF16)
+        for d in range(1, n_y):
+            go(heads_copy(d, h))
+        if h % 2 == 0 and w_done < hops:
+            w_step(w_done)
+            w_done += 1
+    while w_done <= hops:
+        w_step(w_done)
+        w_done += 1
 
     sibling = {"tensor": t + 1 - 2 * c}
     w_all = w[...].reshape(ycols, w.shape[2])
@@ -178,8 +199,10 @@
     for j in range(n_y):
         g = lax.rem(y + n_y - j, n_y)
         if j > 0:
-            heads_copy(j).wait_recv()
-        pr = lax.dot_general(heads[g], w_all, NT, preferred_element_type=F32)
+            for h in range(group):
+                heads_copy(j, h).wait_recv()
+        held = jnp.concatenate([heads[g, h] for h in range(group)], axis=1)
+        pr = lax.dot_general(held, w_all, NT, preferred_element_type=F32)
         pr = pr.astype(BF16).reshape(n_x, 2, trows, ycols)
         a_part[0, g] = pr[:, 0]
         a_part[1, g] = pr[:, 1]
@@ -223,13 +246,31 @@
         square = square + jnp.sum(m_g * m_g, axis=1, keepdims=True)
         mixed.append(m_g)
     scale = lax.rsqrt(square * (1.0 / width) + 1e-05)
+    def cols_copy(d):
+        to = lax.rem(t + d, n_t)
+        return remote(
+            sendn.at[to], zc.at[z, t], n_ss.at[d - 1], n_rs.at[d - 1], {"tensor": to}
+        )
+
+    def logit_copy(d):
+        to = lax.rem(t + d, n_t)
+        return remote(
+            logit_ref.at[t], logit_ref.at[t], l_ss.at[d - 1], l_rs.at[d - 1], {"tensor": to}
+        )
+
+    normed = []
+    for g in range(n_y):
+        n_g = (mixed[g] * scale * gain_ref[:, g * ycols : (g + 1) * ycols]).astype(BF16)
+        for i in range(per):
+            sendn[g * per + i] = n_g[:, i * tcols : (i + 1) * tcols]
+        normed.append(n_g)
+    for d in range(1, n_t):
+        go(cols_copy(d))
+    zc[z, t] = sendn[t]
     logits = None
     for g in range(n_y):
-        normed = (mixed[g] * scale * gain_ref[:, g * ycols : (g + 1) * ycols]).astype(BF16)
-        for i in range(per):
-            sendn[g * per + i] = normed[:, i * tcols : (i + 1) * tcols]
         term = lax.dot_general(
-            normed,
+            normed[g],
             router_ref[:, g * ycols : (g + 1) * ycols],
             NT,
             preferred_element_type=F32,
@@ -240,99 +281,111 @@
     for e in range(router_ref.shape[0]):
         wide = jnp.where(lane == e, logits[:, e : e + 1], wide)
     logit_ref[t] = wide
-    cols_ref[t] = sendn[t]
-
-    def cols_copy(d):
-        to = lax.rem(t + d, n_t)
-        return remote(
-            sendn.at[to], cols_ref.at[t], n_ss.at[d - 1], n_rs.at[d - 1], {"tensor": to}
-        )
-
-    def logit_copy(d):
-        to = lax.rem(t + d, n_t)
-        return remote(
-            logit_ref.at[t], logit_ref.at[t], l_ss.at[d - 1], l_rs.at[d - 1], {"tensor": to}
-        )
-
     for d in range(1, n_t):
-        go(cols_copy(d))
         go(logit_copy(d))
-    for d in range(1, n_t):
-        cols_copy(d).wait_recv()
-        logit_copy(d).wait_recv()
-
-    ids = ids_ref[...]
+
     n_e = table.shape[0]
     expert = lax.broadcasted_iota(jnp.int32, (n_e, rows), 0)
-    named = ids[0:1, :] == expert
-    for j in range(1, ids.shape[0]):
-        named = jnp.logical_or(named, ids[j : j + 1, :] == expert)
+    place = lax.broadcasted_iota(jnp.int32, (n_z, rows), 0)
     earlier = (
         lax.broadcasted_iota(jnp.int32, (rows, rows), 0)
         < lax.broadcasted_iota(jnp.int32, (rows, rows), 1)
     )
-    before = jnp.dot(
-        jnp.where(named, 1.0, 0.0).astype(BF16),
-        jnp.where(earlier, 1.0, 0.0).astype(BF16),
-        preferred_element_type=F32,
-    )
-    table[...] = jnp.where(named, before.astype(jnp.int32), -1)
+    earlier = jnp.where(earlier, 1.0, 0.0).astype(BF16)
+
+    def slots_of(named):
+        before = jnp.dot(
+            jnp.where(named, 1.0, 0.0).astype(BF16), earlier, preferred_element_type=F32
+        )
+        return jnp.where(named, before.astype(jnp.int32), -1)
+
+    for d in range(1, n_z):
+        ids_copy(d).wait_recv()
+    own = ids_all[z]
+    named = own[0:1, :] == expert
+    for j in range(1, own.shape[0]):
+        named = jnp.logical_or(named, own[j : j + 1, :] == expert)
+    table[...] = slots_of(named)
+    named = jnp.zeros((n_z, rows), jnp.int32)
+    for p in range(n_z):
+        ids = ids_all[lax.rem(z + order[p], n_z)]
+        hit = jnp.sum(jnp.where(ids == z, 1, 0), axis=0, keepdims=True)
+        named = jnp.where(place == p, hit, named)
+    mine[...] = slots_of(named > 0)
+    for d in range(1, n_t):
+        cols_copy(d).wait_recv()
+
     slot = lax.broadcasted_iota(jnp.int32, (CAP, rows), 0)
-    cols = cols_ref[...].reshape(rows, tcols)
-
-    def slot_copy(p):
-        to = lax.rem(z + n_z - order[p], n_z)
-        return remote(
-            slots.at[p],
-            xbuf.at[t, pl.ds(p * CAP, CAP)],
-            s_ss.at[p],
-            s_rs.at[p],
-            {"expert": to},
-        )
-
-    for p in range(n_z):
-        e = lax.rem(z + n_z - order[p], n_z)
-        pick = jnp.where(table[pl.ds(e, 1), :] == slot, 1.0, 0.0).astype(BF16)
-        picked = jnp.dot(pick, cols, preferred_element_type=F32).astype(BF16)
-        if p == 0:
-            xbuf[t, 0:CAP] = picked
-        else:
-            slots[p] = picked
-            go(slot_copy(p))
-
-    def share_copy(g, d):
-        ref = xbuf.at[t, pl.ds(g * grows, grows)]
+
+    def z_hop(way, s):
+        block = lax.rem(z + (n_z - s if way == 0 else s), n_z)
+        span = pl.ds(way * (n_t // 2), n_t // 2)
+        ref = zc.at[block, span] if s == hops - 1 else zc.at[block]
+        return remote(
+            ref, ref, s_ss.at[way, s], s_rs.at[way, s], {"expert": right if way == 0 else left}
+        )
+
+    def chunk(held, p):
+        return xbuf.at[held, pl.ds(p * CAP, CAP)]
+
+    def share_copy(p, d):
+        ref = chunk(t, p)
         to = lax.rem(x + d, n_x) * 2 + c
-        return remote(ref, ref, a_ss.at[g, d - 1], a_rs.at[g, d - 1], {"tensor": to})
-
-    def pass_copy(g, d):
-        held = lax.rem(x + n_x - d, n_x) * 2 + c
-        ref = xbuf.at[held, pl.ds(g * grows, grows)]
-        return remote(ref, ref, b_ss.at[g, d], b_rs.at[g, d], {"tensor": sibling_t})
-
-    def share(g):
-        for p in range(g * per_group, (g + 1) * per_group):
-            if p > 0:
-                slot_copy(p).wait_recv()
-        for d in range(1, n_x):
-            go(share_copy(g, d))
-        go(pass_copy(g, 0))
-
-    def forward(g, d):
-        share_copy(g, d).wait_recv()
-        go(pass_copy(g, d))
-
-    def arrive(g, d):
-        pass_copy(g, d).wait_recv()
+        return remote(ref, ref, a_ss.at[p, d - 1], a_rs.at[p, d - 1], {"tensor": to})
+
+    def relay_copy(p):
+        d = near[p % 2]
+        ref = chunk(lax.rem(x + n_x - d, n_x) * 2 + c, p)
+        to = lax.rem(x + d, n_x) * 2 + c
+        return remote(ref, ref, a_ss.at[p, 1], a_rs.at[p, 1], {"tensor": to})
+
+    def pass_copy(p, d):
+        ref = chunk(lax.rem(x + n_x - d, n_x) * 2 + c, p)
+        return remote(ref, ref, b_ss.at[p, d], b_rs.at[p, d], {"tensor": sibling_t})
+
+    def share(p):
+        block = zc[lax.rem(z + order[p], n_z)].reshape(rows, tcols)
+        pick = jnp.where(mine[p : p + 1, :] == slot, 1.0, 0.0).astype(BF16)
+        xbuf[t, p * CAP : (p + 1) * CAP] = jnp.dot(
+            pick, block, preferred_element_type=F32
+        ).astype(BF16)
+        for d in near:
+            go(share_copy(p, d))
+        go(pass_copy(p, 0))
+
+    done = set()
+
+    def relay(p):
+        if ("relay", p) in done:
+            return
+        done.add(("relay", p))
+        for d in near if p % 2 == 0 else near[::-1]:
+            share_copy(p, d).wait_recv()
+            if n_x > 2 and d == near[p % 2]:
+                go(relay_copy(p))
+            go(pass_copy(p, d))
+
+    def far(p):
+        if n_x > 2 and ("far", p) not in done:
+            relay(p)
+            done.add(("far", p))
+            relay_copy(p).wait_recv()
+            go(pass_copy(p, 2))
 
     def gate_up(h, d):
+        for p in range(h * per_half, (h + 1) * per_half):
+            if d in near:
+                relay(p)
+            elif d > 0:
+                far(p)
+            pass_copy(p, d).wait_recv()
         i = lax.rem(x + n_x - d, n_x)
         span = pl.ds(h * hrows, hrows)
         held = jnp.concatenate([xbuf[i * 2, span], xbuf[i * 2 + 1, span]], axis=1)
         g_term = lax.dot_general(held, wg[i], NT, preferred_element_type=F32)
-        act_g[...] = g_term if d == 0 else act_g[...] + g_term
+        act_g[h] = g_term if d == 0 else act_g[h] + g_term
         u_term = lax.dot_general(held, wu[i], NT, preferred_element_type=F32)
-        act_u[...] = u_term if d == 0 else act_u[...] + u_term
+        act_u[h] = u_term if d == 0 else act_u[h] + u_term
 
     def pair_copy(h, d):
         i = lax.rem(x + d, n_x)
@@ -341,30 +394,49 @@
             {"tensor": sibling_t},
         )
 
+    targets = ([2] if n_x > 2 else []) + list(near) + [0]
+
     def down(h):
-        g_all = act_g[...]
-        hidden[...] = (g_all / (1.0 + jnp.exp(-g_all)) * act_u[...]).astype(BF16)
-        for d in list(range(1, n_x)) + [0]:
+        g_all = act_g[h]
+        hidden[...] = (g_all / (1.0 + jnp.exp(-g_all)) * act_u[h]).astype(BF16)
+        for d in targets:
             i = lax.rem(x + d, n_x)
             o = jnp.dot(hidden[...], wd[i], preferred_element_type=F32).astype(BF16)
             part[h, 0, i] = o[:, :tcols]
             part[h, 1, i] = o[:, tcols:]
             go(pair_copy(h, d))
 
-    def cross_copy(h, d):
-        to = lax.rem(x + d, n_x)
-        return remote(
-            part.at[h, c, to], cross.at[h, d - 1], x_ss.at[h, d - 1], x_rs.at[h, d - 1],
-            {"tensor": to * 2 + c},
-        )
-
-    def reduce_send(h):
-        for d in list(range(1, n_x)) + [0]:
-            i = lax.rem(x + d, n_x)
-            pair_copy(h, d).wait_recv()
-            part[h, c, i] = (part[h, c, i].astype(F32) + peer[h, i].astype(F32)).astype(BF16)
-            if d > 0:
-                go(cross_copy(h, d))
+    def pair_sum(h, d):
+        i = lax.rem(x + d, n_x)
+        pair_copy(h, d).wait_recv()
+        part[h, c, i] = (part[h, c, i].astype(F32) + peer[h, i].astype(F32)).astype(BF16)
+
+    def unit(q, d):
+        h = q // units_half
+        span = pl.ds((q % units_half) * urows, urows)
+        return part.at[h, c, lax.rem(x + d, n_x), span]
+
+    def via_copy(q):
+        to = lax.rem(x + near[q % 2], n_x) * 2 + c
+        return remote(unit(q, 2), vbuf.at[q], v_ss.at[q], v_rs.at[q], {"tensor": to})
+
+    def near_copy(q, d):
+        k = near.index(d)
+        to = lax.rem(x + d, n_x) * 2 + c
+        return remote(unit(q, d), cross.at[q, k], x_ss.at[q, k], x_rs.at[q, k], {"tensor": to})
+
+    def sum_first(q):
+        if n_x > 2:
+            go(via_copy(q))
+            go(near_copy(q, near[1 - q % 2]))
+
+    def sum_second(q):
+        d = near[q % 2] if n_x > 2 else 1
+        if n_x > 2:
+            via_copy(q).wait_recv()
+            ref = unit(q, d)
+            ref[...] = (ref[...].astype(F32) + vbuf[q].astype(F32)).astype(BF16)
+        go(near_copy(q, d))
 
     def return_copy(p):
         to = lax.rem(z + order[p], n_z)
@@ -372,14 +444,14 @@
             ybuf.at[p], zbuf.at[pl.ds(p * CAP, CAP)], z_ss.at[p], z_rs.at[p], {"expert": to}
         )
 
-    def reduce_recv(h):
-        total = part[h, c, x].astype(F32)
-        for d in range(1, n_x):
-            cross_copy(h, d).wait_recv()
-            total = total + cross[h, d - 1].astype(F32)
+    def sum_last(q):
+        total = unit(q, 0)[...].astype(F32)
+        for k in range(len(near)):
+            near_copy(q, near[k]).wait_recv()
+            total = total + cross[q, k].astype(F32)
         total = total.astype(BF16)
-        for i in range(per_half):
-            p = h * per_half + i
+        for i in list(range(per_unit))[::-1]:
+            p = q * per_unit + i
             block = total[i * CAP : (i + 1) * CAP]
             if p == 0:
                 zbuf[0:CAP] = block
@@ -387,11 +459,65 @@
                 ybuf[p] = block
                 go(return_copy(p))
 
-    def of_half(h):
-        return range(h * groups_half, (h + 1) * groups_half)
-
-    for g in range(n_groups):
-        share(g)
+    for way in range(2):
+        go(z_hop(way, 0))
+    share(0)
+    fresh, older = [0], []
+    for s in range(1, hops + 1):
+        for way in range(2):
+            z_hop(way, s - 1).wait_recv()
+            if s < hops:
+                go(z_hop(way, s))
+        now = [2 * s - 1, 2 * s] if s < hops else [n_z - 1]
+        for p in now:
+            share(p)
+        if s == 1:
+            for load in loads:
+                load.wait()
+        if s == hops - 1:
+            gate_up(0, 0)
+        for p in fresh:
+            relay(p)
+        for p in older:
+            far(p)
+        fresh, older = now, fresh
+    for d in near:
+        gate_up(0, d)
+    for p in range(n_z - 1):
+        relay(p)
+    if n_x > 2:
+        gate_up(0, 2)
+    relay(n_z - 1)
+    if hops == 1:
+        gate_up(0, 0)
+    gate_up(1, 0)
+    down(0)
+    for d in near:
+        gate_up(1, d)
+    for d in targets:
+        pair_sum(0, d)
+    early = [q for q in range(1, units_half)]
+    middle = list(range(units_half, n_units))
+    for q in early:
+        sum_first(q)
+    for p in range(n_z):
+        far(p)
+    for q in early:
+        sum_second(q)
+    if n_x > 2:
+        gate_up(1, 2)
+    down(1)
+    for d in targets:
+        pair_sum(1, d)
+    for q in middle:
+        sum_first(q)
+    for q in early:
+        sum_last(q)
+    for q in middle:
+        sum_second(q)
+    sum_first(0)
+    for d in range(1, n_t):
+        logit_copy(d).wait_recv()
     gates = jnp.transpose(logit_ref[...].reshape(rows, 128))[0:n_e]
     gates = 1.0 / (1.0 + jnp.exp(-gates))
     pieces = []
@@ -404,20 +530,10 @@
     high = comb.astype(BF16)
     comb_hi[...] = high
     comb_lo[...] = (comb - high.astype(F32)).astype(BF16)
-    for load in loads:
-        load.wait()
-    for h in range(halves):
-        for d in list(range(0, n_x)):
-            for g in of_half(h):
-                if d > 0:
-                    forward(g, d)
-            for g in of_half(h):
-                arrive(g, d)
-            gate_up(h, d)
-        down(h)
-        reduce_send(h)
-    for h in range(halves):
-        reduce_recv(h)
+    sum_second(0)
+    for q in middle:
+        sum_last(q)
+    sum_last(0)
     for p in range(1, n_z):
         return_copy(p).wait_recv()
 
@@ -446,7 +562,7 @@
 
 def slot_order(n_z):
     if n_z == 8:
-        return (0, 1, 7, 2, 6, 3, 5, 4)
+        return (0, 7, 1, 6, 2, 5, 3, 4)
     return tuple(range(n_z))
 
 
@@ -463,7 +579,11 @@
     top = expert_ids.shape[2]
     ycols, tcols, trows, xcols = width // n_y, width // n_t, rows // n_t, width // n_x
     wcols = out_weight.shape[1]
-    hrows = n_z // 2 * CAP
+    group = qcols // HEAD_WIDTH
+    ny1 = max(1, n_y - 1)
+    n_units = 4 if n_z % 4 == 0 else 2
+    len_near = 2 if n_x > 2 else 1
+    hrows, urows = n_z // 2 * CAP, n_z // n_units * CAP
     hbm = pl.BlockSpec(memory_space=pltpu.HBM)
     dma = pltpu.SemaphoreType.DMA
     V = pltpu.VMEM
@@ -478,14 +598,14 @@
             V((rows, qcols), BF16),
             V((1, width), F32),
             V((n_e, width), BF16),
-            V((top, rows), jnp.int32),
+            V((n_z, top, rows), jnp.int32),
             V((trows, width), F32),
-            V((n_t, trows, tcols), BF16),
+            V((n_z, n_t, trows, tcols), BF16),
             V((n_t, trows, 128), F32),
             V((n_z, 2, rows, HEAD_WIDTH), BF16),
             V((n_z, wcols, qcols), BF16),
             V((n_z, qcols // HEAD_WIDTH, rows, rows), F32),
-            V((n_y, rows, qcols), BF16),
+            V((n_y, qcols // HEAD_WIDTH, rows, HEAD_WIDTH), BF16),
             V((2, n_y, n_x, trows, ycols), BF16),
             V((n_y, n_x, trows, ycols), BF16),
             V((n_x, n_y, trows, ycols), BF16),
@@ -497,15 +617,16 @@
             V((n_x, ff, xcols), BF16),
             V((n_x, ff, xcols), BF16),
             V((n_x, ff, xcols), BF16),
-            V((n_z, CAP, tcols), BF16),
             V((n_t, n_z * CAP, tcols), BF16),
             V((n_e, rows), jnp.int32),
+            V((n_z, rows), jnp.int32),
             V((hrows, ff), BF16),
-            V((hrows, ff), F32),
-            V((hrows, ff), F32),
+            V((2, hrows, ff), F32),
+            V((2, hrows, ff), F32),
             V((2, 2, n_x, hrows, tcols), BF16),
             V((2, n_x, hrows, tcols), BF16),
-            V((2, n_x - 1, hrows, tcols), BF16),
+            V((n_units, urows, tcols), BF16),
+            V((n_units, len_near, urows, tcols), BF16),
             V((n_z, CAP, tcols), BF16),
             V((n_z * CAP, tcols), BF16),
             V((rows, n_z * CAP), BF16),
@@ -514,13 +635,14 @@
             V((n_t, trows, tcols), BF16),
             dma((7,)), dma,
             dma((2, hops)), dma((2, hops)), dma((2, hops)), dma((2, hops)),
-            dma((n_y - 1,)), dma((n_y - 1,)), dma((n_y,)), dma((n_y,)),
-            dma((n_x - 1,)), dma((n_x - 1,)), dma((n_y - 1,)), dma((n_y - 1,)),
+            dma((ny1, group)), dma((ny1, group)), dma((n_y,)), dma((n_y,)),
+            dma((n_x - 1,)), dma((n_x - 1,)), dma((ny1,)), dma((ny1,)),
             dma((n_t - 1,)), dma((n_t - 1,)), dma((n_t - 1,)), dma((n_t - 1,)),
-            dma((3, n_x)),
-            dma((n_z,)), dma((n_z,)),
-            dma((4, n_x - 1)), dma((4, n_x - 1)), dma((4, n_x)), dma((4, n_x)),
-            dma((2, n_x)), dma((2, n_x)), dma((2, n_x - 1)), dma((2, n_x - 1)),
+            dma((n_z - 1,)), dma((n_z - 1,)),
+            dma((3, n_x)), dma((2, hops)), dma((2, hops)),
+            dma((n_z, 3)), dma((n_z, 3)), dma((n_z, n_x)), dma((n_z, n_x)),
+            dma((2, n_x)), dma((2, n_x)), dma((n_units,)), dma((n_units,)),
+            dma((n_units, len_near)), dma((n_units, len_near)),
             dma((n_z,)), dma((n_z,)), dma((n_t - 1,)), dma((n_t - 1,)),
         ],
         compiler_params=pltpu.CompilerParams(

time: 118 us -> 121 us (1.025); the launches traced: 116 us -> 121 us
  Pallas kernels: 115 us -> 119 us
    pallas_call x1, Pallas kernels: 115 us -> 119 us  [local(): pl.pallas_call(functools.partial(block_kernel, n_y, n_z, n_t, slot_order(...]
where the time goes in v3:
time: 121 us
  Pallas kernels  119 us (98%)
  local copies, waits for them, and re-layouts  1.54 us (1%)
    pallas_call x1, Pallas kernels, local(): pl.pallas_call(functools.partial(block_kernel, n_y, n_z, n_t, slot_order(...  119 us

profile of v3, /device:TPU:1, one launch (start us, length us, event | category | flops | bytes accessed | tf_op | source)
XLA Modules:
  0.0 120.8 jit_solution(108205978157164424)
XLA Ops:
  0.0 119.2 %shard_map.109 = bf16[16,3072]{1,0:T(8,128)(2,1)} custom-call(bf16[128,384]{1,0:T(8,128)(2,1)} %bitcast.23, bf16[128,128]{1,0:T(8,128)(2,1)} %bitcast.26, bf16[128,128]{1,0:T(8,128)(2,1)} %bitcast.27, bf16[96,384]{1,0:T(8,128)(2,1)} %bitcast.24, bf16[128,3072]{1,0:T(8,128)(2,1)} %bitcast.21, f32[1,3072]{1,0:T(1,128)} %bitcast.28, bf16[8,3072]{1,0:T(8,128)(2,1)} %bitcast.25, ...), custom_call_target="tpu_custom_call" | custom-call | tf_op jit(solution)/shard_map/pallas_call | solution.py:592
  119.2 1.5 %copy.13 = bf16[1,16,3072]{2,1,0:T(8,128)(2,1)} copy(bf16[1,16,3072]{2,1,0:T(8,128)(2,1)} %bitcast.22) | data formatting | bytes 196608

commit v4 on v2

--- a/solution.py
+++ b/solution.py
@@ -58,10 +58,12 @@
     half = w_ref.shape[0] // 2
     halves = 2
     per_half = n_z // halves
-    n_groups = 4 if n_z % 4 == 0 else 2
-    per_group = n_z // n_groups
-    groups_half = n_groups // halves
-    hrows, grows = per_half * CAP, per_group * CAP
+    n_units = 4 if n_z % 4 == 0 else 2
+    per_unit = n_z // n_units
+    units_half = n_units // halves
+    hrows, urows = per_half * CAP, per_unit * CAP
+    near = (1, n_x - 1) if n_x > 2 else (1,)
+    others = near + ((2,) if n_x > 2 else ())
     sibling_t = t + 1 - 2 * c
     sent = []
 
@@ -145,6 +147,12 @@
         kv_hop(way, hops - 1).wait_recv()
     score(lax.rem(z + hops, n_z))
 
+    def heads_copy(d, h):
+        return remote(
+            heads.at[y, h], heads.at[y, h], h_ss.at[d - 1, h], h_rs.at[d - 1, h],
+            {"dp": lax.rem(y + d, n_y)},
+        )
+
     all_values = kv[:, 1].reshape(n_z * rows, HEAD_WIDTH)
     shape = (rows, n_z * rows)
     causal = lax.broadcasted_iota(jnp.int32, shape, 1) <= (
@@ -156,15 +164,9 @@
         e_h = jnp.exp(s_h - jnp.max(s_h, axis=1, keepdims=True))
         a_h = (e_h * (1.0 / jnp.sum(e_h, axis=1, keepdims=True))).astype(BF16)
         o_h = jnp.dot(a_h, all_values, preferred_element_type=F32)
-        heads[y, :, h * HEAD_WIDTH : (h + 1) * HEAD_WIDTH] = o_h.astype(BF16)
-
-    def heads_copy(d):
-        return remote(
-            heads.at[y], heads.at[y], h_ss.at[d - 1], h_rs.at[d - 1], {"dp": lax.rem(y + d, n_y)}
-        )
-
-    for d in range(1, n_y):
-        go(heads_copy(d))
+        heads[y, h] = o_h.astype(BF16)
+        for d in range(1, n_y):
+            go(heads_copy(d, h))
     for way in range(2):
         w_hop(way, hops - 1).wait_recv()
 
@@ -178,8 +180,10 @@
     for j in range(n_y):
         g = lax.rem(y + n_y - j, n_y)
         if j > 0:
-            heads_copy(j).wait_recv()
-        pr = lax.dot_general(heads[g], w_all, NT, preferred_element_type=F32)
+            for h in range(group):
+                heads_copy(j, h).wait_recv()
+        held = jnp.concatenate([heads[g, h] for h in range(group)], axis=1)
+        pr = lax.dot_general(held, w_all, NT, preferred_element_type=F32)
         pr = pr.astype(BF16).reshape(n_x, 2, trows, ycols)
         a_part[0, g] = pr[:, 0]
         a_part[1, g] = pr[:, 1]
@@ -223,13 +227,31 @@
         square = square + jnp.sum(m_g * m_g, axis=1, keepdims=True)
         mixed.append(m_g)
     scale = lax.rsqrt(square * (1.0 / width) + 1e-05)
+    def cols_copy(d):
+        to = lax.rem(t + d, n_t)
+        return remote(
+            sendn.at[to], cols_ref.at[t], n_ss.at[d - 1], n_rs.at[d - 1], {"tensor": to}
+        )
+
+    def logit_copy(d):
+        to = lax.rem(t + d, n_t)
+        return remote(
+            logit_ref.at[t], logit_ref.at[t], l_ss.at[d - 1], l_rs.at[d - 1], {"tensor": to}
+        )
+
+    normed = []
+    for g in range(n_y):
+        n_g = (mixed[g] * scale * gain_ref[:, g * ycols : (g + 1) * ycols]).astype(BF16)
+        for i in range(per):
+            sendn[g * per + i] = n_g[:, i * tcols : (i + 1) * tcols]
+        normed.append(n_g)
+    for d in range(1, n_t):
+        go(cols_copy(d))
+    cols_ref[t] = sendn[t]
     logits = None
     for g in range(n_y):
-        normed = (mixed[g] * scale * gain_ref[:, g * ycols : (g + 1) * ycols]).astype(BF16)
-        for i in range(per):
-            sendn[g * per + i] = normed[:, i * tcols : (i + 1) * tcols]
         term = lax.dot_general(
-            normed,
+            normed[g],
             router_ref[:, g * ycols : (g + 1) * ycols],
             NT,
             preferred_element_type=F32,
@@ -240,30 +262,12 @@
     for e in range(router_ref.shape[0]):
         wide = jnp.where(lane == e, logits[:, e : e + 1], wide)
     logit_ref[t] = wide
-    cols_ref[t] = sendn[t]
-
-    def cols_copy(d):
-        to = lax.rem(t + d, n_t)
-        return remote(
-            sendn.at[to], cols_ref.at[t], n_ss.at[d - 1], n_rs.at[d - 1], {"tensor": to}
-        )
-
-    def logit_copy(d):
-        to = lax.rem(t + d, n_t)
-        return remote(
-            logit_ref.at[t], logit_ref.at[t], l_ss.at[d - 1], l_rs.at[d - 1], {"tensor": to}
-        )
-
     for d in range(1, n_t):
-        go(cols_copy(d))
         go(logit_copy(d))
-    for d in range(1, n_t):
-        cols_copy(d).wait_recv()
-        logit_copy(d).wait_recv()
-
-    ids = ids_ref[...]
+
     n_e = table.shape[0]
     expert = lax.broadcasted_iota(jnp.int32, (n_e, rows), 0)
+    ids = ids_ref[...]
     named = ids[0:1, :] == expert
     for j in range(1, ids.shape[0]):
         named = jnp.logical_or(named, ids[j : j + 1, :] == expert)
@@ -277,94 +281,102 @@
         preferred_element_type=F32,
     )
     table[...] = jnp.where(named, before.astype(jnp.int32), -1)
+    for d in range(1, n_t):
+        cols_copy(d).wait_recv()
+
     slot = lax.broadcasted_iota(jnp.int32, (CAP, rows), 0)
     cols = cols_ref[...].reshape(rows, tcols)
 
+    def chunk(held, p):
+        return xbuf.at[held, pl.ds(p * CAP, CAP)]
+
     def slot_copy(p):
         to = lax.rem(z + n_z - order[p], n_z)
-        return remote(
-            slots.at[p],
-            xbuf.at[t, pl.ds(p * CAP, CAP)],
-            s_ss.at[p],
-            s_rs.at[p],
-            {"expert": to},
-        )
-
-    for p in range(n_z):
+        return remote(slots.at[p], chunk(t, p), s_ss.at[p], s_rs.at[p], {"expert": to})
+
+    def pick(p):
         e = lax.rem(z + n_z - order[p], n_z)
-        pick = jnp.where(table[pl.ds(e, 1), :] == slot, 1.0, 0.0).astype(BF16)
-        picked = jnp.dot(pick, cols, preferred_element_type=F32).astype(BF16)
+        hot = jnp.where(table[pl.ds(e, 1), :] == slot, 1.0, 0.0).astype(BF16)
+        picked = jnp.dot(hot, cols, preferred_element_type=F32).astype(BF16)
         if p == 0:
             xbuf[t, 0:CAP] = picked
         else:
             slots[p] = picked
             go(slot_copy(p))
 
-    def share_copy(g, d):
-        ref = xbuf.at[t, pl.ds(g * grows, grows)]
+    def share_copy(p, d):
+        ref = chunk(t, p)
         to = lax.rem(x + d, n_x) * 2 + c
-        return remote(ref, ref, a_ss.at[g, d - 1], a_rs.at[g, d - 1], {"tensor": to})
-
-    def pass_copy(g, d):
-        held = lax.rem(x + n_x - d, n_x) * 2 + c
-        ref = xbuf.at[held, pl.ds(g * grows, grows)]
-        return remote(ref, ref, b_ss.at[g, d], b_rs.at[g, d], {"tensor": sibling_t})
-
-    def share(g):
-        for p in range(g * per_group, (g + 1) * per_group):
-            if p > 0:
-                slot_copy(p).wait_recv()
-        for d in range(1, n_x):
-            go(share_copy(g, d))
-        go(pass_copy(g, 0))
-
-    def forward(g, d):
-        share_copy(g, d).wait_recv()
-        go(pass_copy(g, d))
-
-    def arrive(g, d):
-        pass_copy(g, d).wait_recv()
+        return remote(ref, ref, a_ss.at[p, d - 1], a_rs.at[p, d - 1], {"tensor": to})
+
+    def pass_copy(p, d):
+        ref = chunk(lax.rem(x + n_x - d, n_x) * 2 + c, p)
+        return remote(ref, ref, b_ss.at[p, d], b_rs.at[p, d], {"tensor": sibling_t})
+
+    def share(p):
+        if p > 0:
+            slot_copy(p).wait_recv()
+        for d in others:
+            go(share_copy(p, d))
+        go(pass_copy(p, 0))
+
+    def forward(p, d):
+        share_copy(p, d).wait_recv()
+        go(pass_copy(p, d))
+
+    def of_half(h):
+        return range(h * per_half, (h + 1) * per_half)
 
     def gate_up(h, d):
+        for p in of_half(h):
+            pass_copy(p, d).wait_recv()
         i = lax.rem(x + n_x - d, n_x)
         span = pl.ds(h * hrows, hrows)
         held = jnp.concatenate([xbuf[i * 2, span], xbuf[i * 2 + 1, span]], axis=1)
         g_term = lax.dot_general(held, wg[i], NT, preferred_element_type=F32)
-        act_g[...] = g_term if d == 0 else act_g[...] + g_term
+        act_g[h] = g_term if d == 0 else act_g[h] + g_term
         u_term = lax.dot_general(held, wu[i], NT, preferred_element_type=F32)
-        act_u[...] = u_term if d == 0 else act_u[...] + u_term
-
-    def pair_copy(h, d):
+        act_u[h] = u_term if d == 0 else act_u[h] + u_term
+
+    def pair_copy(q, d):
         i = lax.rem(x + d, n_x)
         return remote(
-            part.at[h, 1 - c, i], peer.at[h, i], p_ss.at[h, d], p_rs.at[h, d],
+            part.at[q, 1 - c, i], peer.at[q, i], p_ss.at[q, d], p_rs.at[q, d],
             {"tensor": sibling_t},
         )
 
-    def down(h):
-        g_all = act_g[...]
-        hidden[...] = (g_all / (1.0 + jnp.exp(-g_all)) * act_u[...]).astype(BF16)
-        for d in list(range(1, n_x)) + [0]:
+    targets = others[::-1] + (0,)
+
+    def activate(h):
+        g_all = act_g[h]
+        hidden[...] = (g_all / (1.0 + jnp.exp(-g_all)) * act_u[h]).astype(BF16)
+
+    def down(first, last):
+        base = first % units_half
+        held = hidden[base * urows : (base + last - first) * urows]
+        for d in targets:
             i = lax.rem(x + d, n_x)
-            o = jnp.dot(hidden[...], wd[i], preferred_element_type=F32).astype(BF16)
-            part[h, 0, i] = o[:, :tcols]
-            part[h, 1, i] = o[:, tcols:]
-            go(pair_copy(h, d))
-
-    def cross_copy(h, d):
+            o = jnp.dot(held, wd[i], preferred_element_type=F32).astype(BF16)
+            for q in range(first, last):
+                o_q = o[(q - first) * urows : (q - first + 1) * urows]
+                part[q, 0, i] = o_q[:, :tcols]
+                part[q, 1, i] = o_q[:, tcols:]
+                go(pair_copy(q, d))
+
+    def cross_copy(q, d):
         to = lax.rem(x + d, n_x)
         return remote(
-            part.at[h, c, to], cross.at[h, d - 1], x_ss.at[h, d - 1], x_rs.at[h, d - 1],
+            part.at[q, c, to], cross.at[q, d - 1], x_ss.at[q, d - 1], x_rs.at[q, d - 1],
             {"tensor": to * 2 + c},
         )
 
-    def reduce_send(h):
-        for d in list(range(1, n_x)) + [0]:
+    def reduce_send(q):
+        for d in targets:
             i = lax.rem(x + d, n_x)
-            pair_copy(h, d).wait_recv()
-            part[h, c, i] = (part[h, c, i].astype(F32) + peer[h, i].astype(F32)).astype(BF16)
+            pair_copy(q, d).wait_recv()
+            part[q, c, i] = (part[q, c, i].astype(F32) + peer[q, i].astype(F32)).astype(BF16)
             if d > 0:
-                go(cross_copy(h, d))
+                go(cross_copy(q, d))
 
     def return_copy(p):
         to = lax.rem(z + order[p], n_z)
@@ -372,14 +384,14 @@
             ybuf.at[p], zbuf.at[pl.ds(p * CAP, CAP)], z_ss.at[p], z_rs.at[p], {"expert": to}
         )
 
-    def reduce_recv(h):
-        total = part[h, c, x].astype(F32)
-        for d in range(1, n_x):
-            cross_copy(h, d).wait_recv()
-            total = total + cross[h, d - 1].astype(F32)
+    def reduce_recv(q):
+        total = part[q, c, x].astype(F32)
+        for d in near + others[len(near) :]:
+            cross_copy(q, d).wait_recv()
+            total = total + cross[q, d - 1].astype(F32)
         total = total.astype(BF16)
-        for i in range(per_half):
-            p = h * per_half + i
+        for i in range(per_unit)[::-1]:
+            p = q * per_unit + i
             block = total[i * CAP : (i + 1) * CAP]
             if p == 0:
                 zbuf[0:CAP] = block
@@ -387,37 +399,62 @@
                 ybuf[p] = block
                 go(return_copy(p))
 
-    def of_half(h):
-        return range(h * groups_half, (h + 1) * groups_half)
-
-    for g in range(n_groups):
-        share(g)
+    for p in range(1, min(3, n_z)):
+        pick(p)
+    pick(0)
+    share(0)
+    for p in range(3, n_z):
+        pick(p)
+    for load in loads:
+        load.wait()
+    for p in range(1, n_z):
+        share(p)
+    gate_up(0, 0)
+    for d in near:
+        for p in of_half(0):
+            forward(p, d)
+    gate_up(1, 0)
+    for d in near:
+        gate_up(0, d)
+    for d in others[len(near) :]:
+        for p in of_half(0):
+            forward(p, d)
+        gate_up(0, d)
+    activate(0)
+    down(0, units_half)
+    for d in near:
+        for p in of_half(1):
+            forward(p, d)
+    for q in range(units_half)[::-1]:
+        reduce_send(q)
+    for d in near:
+        gate_up(1, d)
+    for d in others[len(near) :]:
+        for p in of_half(1):
+            forward(p, d)
+        gate_up(1, d)
+    activate(1)
+    for q in range(units_half, n_units)[::-1]:
+        down(q, q + 1)
+        reduce_send(q)
+    for q in range(units_half)[::-1]:
+        reduce_recv(q)
+    for d in range(1, n_t):
+        logit_copy(d).wait_recv()
     gates = jnp.transpose(logit_ref[...].reshape(rows, 128))[0:n_e]
     gates = 1.0 / (1.0 + jnp.exp(-gates))
     pieces = []
     for p in range(n_z):
         e = lax.rem(z + n_z - order[p], n_z)
-        pick = jnp.where(expert == e, gates, 0.0)
-        pick = jnp.sum(pick, axis=0, keepdims=True)
-        pieces.append(jnp.where(table[pl.ds(e, 1), :] == slot, pick, 0.0))
+        gate = jnp.where(expert == e, gates, 0.0)
+        gate = jnp.sum(gate, axis=0, keepdims=True)
+        pieces.append(jnp.where(table[pl.ds(e, 1), :] == slot, gate, 0.0))
     comb = jnp.transpose(jnp.concatenate(pieces, axis=0))
     high = comb.astype(BF16)
     comb_hi[...] = high
     comb_lo[...] = (comb - high.astype(F32)).astype(BF16)
-    for load in loads:
-        load.wait()
-    for h in range(halves):
-        for d in list(range(0, n_x)):
-            for g in of_half(h):
-                if d > 0:
-                    forward(g, d)
-            for g in of_half(h):
-                arrive(g, d)
-            gate_up(h, d)
-        down(h)
-        reduce_send(h)
-    for h in range(halves):
-        reduce_recv(h)
+    for q in range(units_half, n_units)[::-1]:
+        reduce_recv(q)
     for p in range(1, n_z):
         return_copy(p).wait_recv()
 
@@ -463,7 +500,9 @@
     top = expert_ids.shape[2]
     ycols, tcols, trows, xcols = width // n_y, width // n_t, rows // n_t, width // n_x
     wcols = out_weight.shape[1]
-    hrows = n_z // 2 * CAP
+    group = qcols // HEAD_WIDTH
+    n_units = 4 if n_z % 4 == 0 else 2
+    hrows, urows = n_z // 2 * CAP, n_z // n_units * CAP
     hbm = pl.BlockSpec(memory_space=pltpu.HBM)
     dma = pltpu.SemaphoreType.DMA
     V = pltpu.VMEM
@@ -485,7 +524,7 @@
             V((n_z, 2, rows, HEAD_WIDTH), BF16),
             V((n_z, wcols, qcols), BF16),
             V((n_z, qcols // HEAD_WIDTH, rows, rows), F32),
-            V((n_y, rows, qcols), BF16),
+            V((n_y, group, rows, HEAD_WIDTH), BF16),
             V((2, n_y, n_x, trows, ycols), BF16),
             V((n_y, n_x, trows, ycols), BF16),
             V((n_x, n_y, trows, ycols), BF16),
@@ -501,11 +540,11 @@
             V((n_t, n_z * CAP, tcols), BF16),
             V((n_e, rows), jnp.int32),
             V((hrows, ff), BF16),
-            V((hrows, ff), F32),
-            V((hrows, ff), F32),
-            V((2, 2, n_x, hrows, tcols), BF16),
-            V((2, n_x, hrows, tcols), BF16),
-            V((2, n_x - 1, hrows, tcols), BF16),
+            V((2, hrows, ff), F32),
+            V((2, hrows, ff), F32),
+            V((n_units, 2, n_x, urows, tcols), BF16),
+            V((n_units, n_x, urows, tcols), BF16),
+            V((n_units, n_x - 1, urows, tcols), BF16),
             V((n_z, CAP, tcols), BF16),
             V((n_z * CAP, tcols), BF16),
             V((rows, n_z * CAP), BF16),
@@ -514,13 +553,14 @@
             V((n_t, trows, tcols), BF16),
             dma((7,)), dma,
             dma((2, hops)), dma((2, hops)), dma((2, hops)), dma((2, hops)),
-            dma((n_y - 1,)), dma((n_y - 1,)), dma((n_y,)), dma((n_y,)),
+            dma((n_y - 1, group)), dma((n_y - 1, group)), dma((n_y,)), dma((n_y,)),
             dma((n_x - 1,)), dma((n_x - 1,)), dma((n_y - 1,)), dma((n_y - 1,)),
             dma((n_t - 1,)), dma((n_t - 1,)), dma((n_t - 1,)), dma((n_t - 1,)),
             dma((3, n_x)),
             dma((n_z,)), dma((n_z,)),
-            dma((4, n_x - 1)), dma((4, n_x - 1)), dma((4, n_x)), dma((4, n_x)),
-            dma((2, n_x)), dma((2, n_x)), dma((2, n_x - 1)), dma((2, n_x - 1)),
+            dma((n_z, n_x - 1)), dma((n_z, n_x - 1)), dma((n_z, n_x)), dma((n_z, n_x)),
+            dma((n_units, n_x)), dma((n_units, n_x)),
+            dma((n_units, n_x - 1)), dma((n_units, n_x - 1)),
             dma((n_z,)), dma((n_z,)), dma((n_t - 1,)), dma((n_t - 1,)),
         ],
         compiler_params=pltpu.CompilerParams(

time: 118 us -> 110 us (0.932); the launches traced: 116 us -> 110 us
  Pallas kernels: 115 us -> 109 us
    pallas_call x1, Pallas kernels: 115 us -> 109 us  [local(): pl.pallas_call(functools.partial(block_kernel, n_y, n_z, n_t, slot_order(...]
where the time goes in v4:
time: 110 us
  Pallas kernels  109 us (99%)
  local copies, waits for them, and re-layouts  1.54 us (1%)
    pallas_call x1, Pallas kernels, local(): pl.pallas_call(functools.partial(block_kernel, n_y, n_z, n_t, slot_order(...  109 us

profile of v4, /device:TPU:1, one launch (start us, length us, event | category | flops | bytes accessed | tf_op | source)
XLA Modules:
  0.0 110.3 jit_solution(17188807196943280518)
XLA Ops:
  0.0 108.7 %shard_map.109 = bf16[16,3072]{1,0:T(8,128)(2,1)} custom-call(bf16[128,384]{1,0:T(8,128)(2,1)} %bitcast.23, bf16[128,128]{1,0:T(8,128)(2,1)} %bitcast.26, bf16[128,128]{1,0:T(8,128)(2,1)} %bitcast.27, bf16[96,384]{1,0:T(8,128)(2,1)} %bitcast.24, bf16[128,3072]{1,0:T(8,128)(2,1)} %bitcast.21, f32[1,3072]{1,0:T(1,128)} %bitcast.28, bf16[8,3072]{1,0:T(8,128)(2,1)} %bitcast.25, ...), custom_call_target="tpu_custom_call" | custom-call | tf_op jit(solution)/shard_map/pallas_call | solution.py:511
  108.7 1.5 %copy.13 = bf16[1,16,3072]{2,1,0:T(8,128)(2,1)} copy(bf16[1,16,3072]{2,1,0:T(8,128)(2,1)} %bitcast.22) | data formatting | bytes 196608

commit v5 on v4

--- a/solution.py
+++ b/solution.py
@@ -177,7 +177,23 @@
         g = lax.rem(y + n_y - j, n_y)
         return remote(a_part.at[1 - c, g], a_peer.at[g], ap_ss.at[j], ap_rs.at[j], sibling)
 
-    for j in range(n_y):
+    def head_cross(d, j):
+        to = lax.rem(x + d, n_x)
+        g = lax.rem(y + n_y - j, n_y)
+        return remote(
+            a_sums.at[to, g], a_cross.at[d - 1, g], ax_ss.at[d - 1, j], ax_rs.at[d - 1, j],
+            {"tensor": to * 2 + c},
+        )
+
+    def head_sum(j):
+        g = lax.rem(y + n_y - j, n_y)
+        head_pair(j).wait_recv()
+        a_sums[:, g] = (a_part[c, g].astype(F32) + a_peer[g].astype(F32)).astype(BF16)
+        for d in others[::-1]:
+            go(head_cross(d, j))
+
+    turns = [0] + sorted(range(1, n_y), key=lambda d: min(d, n_y - d))
+    for k, j in enumerate(turns):
         g = lax.rem(y + n_y - j, n_y)
         if j > 0:
             for h in range(group):
@@ -188,32 +204,25 @@
         a_part[0, g] = pr[:, 0]
         a_part[1, g] = pr[:, 1]
         go(head_pair(j))
-    for j in range(n_y):
-        g = lax.rem(y + n_y - j, n_y)
-        head_pair(j).wait_recv()
-        a_sums[:, g] = (a_part[c, g].astype(F32) + a_peer[g].astype(F32)).astype(BF16)
-
-    def head_cross(d):
-        to = lax.rem(x + d, n_x)
-        return remote(
-            a_sums.at[to], a_cross.at[d - 1], ax_ss.at[d - 1], ax_rs.at[d - 1], {"tensor": to * 2 + c}
-        )
-
-    for d in range(1, n_x):
-        go(head_cross(d))
-    total = a_sums[x].astype(F32)
-    for d in range(1, n_x):
-        head_cross(d).wait_recv()
-        total = total + a_cross[d - 1].astype(F32)
-    att[...] = total.astype(BF16)
+        if k > 0:
+            head_sum(turns[k - 1])
+    head_sum(turns[-1])
 
     def back_copy(d):
         to = lax.rem(y + d, n_y)
         return remote(att.at[to], attn.at[y], y_ss.at[d - 1], y_rs.at[d - 1], {"dp": to})
 
-    for d in range(1, n_y):
-        go(back_copy(d))
-    attn[y] = att[y]
+    for j in turns:
+        g = lax.rem(y + n_y - j, n_y)
+        total = a_sums[x, g].astype(F32)
+        for d in others:
+            head_cross(d, j).wait_recv()
+            total = total + a_cross[d - 1, g].astype(F32)
+        if j == 0:
+            attn[y] = total.astype(BF16)
+        else:
+            att[g] = total.astype(BF16)
+            go(back_copy(n_y - j))
     for copy in later:
         copy.wait()
     for d in range(1, n_y):
@@ -554,7 +563,7 @@
             dma((7,)), dma,
             dma((2, hops)), dma((2, hops)), dma((2, hops)), dma((2, hops)),
             dma((n_y - 1, group)), dma((n_y - 1, group)), dma((n_y,)), dma((n_y,)),
-            dma((n_x - 1,)), dma((n_x - 1,)), dma((n_y - 1,)), dma((n_y - 1,)),
+            dma((n_x - 1, n_y)), dma((n_x - 1, n_y)), dma((n_y - 1,)), dma((n_y - 1,)),
             dma((n_t - 1,)), dma((n_t - 1,)), dma((n_t - 1,)), dma((n_t - 1,)),
             dma((3, n_x)),
             dma((n_z,)), dma((n_z,)),

time: 110 us -> 109 us (level)
  Pallas kernels: 109 us -> 107 us
    pallas_call x1, Pallas kernels: 109 us -> 107 us  [local(): pl.pallas_call(functools.partial(block_kernel, n_y, n_z, n_t, slot_order(...]
where the time goes in v5:
time: 109 us; the launch traced here: 108 us
  Pallas kernels  107 us (98%)
  local copies, waits for them, and re-layouts  1.54 us (1%)
    pallas_call x1, Pallas kernels, local(): pl.pallas_call(functools.partial(block_kernel, n_y, n_z, n_t, slot_order(...  107 us

profile of v5, /device:TPU:1, one launch (start us, length us, event | category | flops | bytes accessed | tf_op | source)
XLA Modules:
  0.0 108.5 jit_solution(14652178569286705253)
XLA Ops:
  0.0 106.9 %shard_map.109 = bf16[16,3072]{1,0:T(8,128)(2,1)} custom-call(bf16[128,384]{1,0:T(8,128)(2,1)} %bitcast.23, bf16[128,128]{1,0:T(8,128)(2,1)} %bitcast.26, bf16[128,128]{1,0:T(8,128)(2,1)} %bitcast.27, bf16[96,384]{1,0:T(8,128)(2,1)} %bitcast.24, bf16[128,3072]{1,0:T(8,128)(2,1)} %bitcast.21, f32[1,3072]{1,0:T(1,128)} %bitcast.28, bf16[8,3072]{1,0:T(8,128)(2,1)} %bitcast.25, ...), custom_call_target="tpu_custom_call" | custom-call | tf_op jit(solution)/shard_map/pallas_call | solution.py:520
  106.9 1.5 %copy.13 = bf16[1,16,3072]{2,1,0:T(8,128)(2,1)} copy(bf16[1,16,3072]{2,1,0:T(8,128)(2,1)} %bitcast.22) | data formatting | bytes 196608

commit v6 on v5

--- a/solution.py
+++ b/solution.py
@@ -38,9 +38,8 @@
     q_hbm, k_ref, v_ref, w_ref, resid_ref, gain_hbm, router_hbm, ids_hbm, wg_ref, wu_ref, wd_ref,
     out_ref,
     q_ref, gain_ref, router_ref, ids_ref, mixed_ref, cols_ref, logit_ref,
-    kv, w, scores, heads, a_part, a_peer, a_sums, a_cross, att, attn, res, sendn,
-    wg, wu, wd, slots, xbuf, table, hidden, act_g, act_u, part, peer, cross, ybuf, zbuf, comb_hi,
-    comb_lo, mix, fin,
+    kv, w, heads, a_part, a_peer, a_sums, a_cross, att, attn, res, sendn,
+    wg, wu, wd, slots, xbuf, table, hidden, act_g, act_u, part, peer, cross, ybuf, zbuf, mix, fin,
     in_sem, res_sem,
     kv_ss, kv_rs, w_ss, w_rs, h_ss, h_rs, ap_ss, ap_rs, ax_ss, ax_rs, y_ss, y_rs,
     n_ss, n_rs, l_ss, l_rs,
@@ -108,44 +107,65 @@
 
     hops = n_z // 2
 
-    def kv_hop(way, s):
+    def hop(way, s, piece):
         block = lax.rem(z + (n_z - s if way == 0 else s), n_z)
-        ref = kv.at[block, way] if s == hops - 1 else kv.at[block]
-        return remote(
-            ref, ref, kv_ss.at[way, s], kv_rs.at[way, s], {"expert": right if way == 0 else left}
-        )
-
-    def w_hop(way, s):
-        block = lax.rem(z + (n_z - s if way == 0 else s), n_z)
-        ref = w.at[block, pl.ds(way * half, half)] if s == hops - 1 else w.at[block]
-        return remote(
-            ref, ref, w_ss.at[way, s], w_rs.at[way, s], {"expert": right if way == 0 else left}
-        )
-
-    def score(block):
+        if piece < 2:
+            ref, sems = kv.at[block, piece], (kv_ss, kv_rs)
+        else:
+            ref, sems = w.at[block, pl.ds((piece - 2) * half, half)], (w_ss, w_rs)
+        return remote(
+            ref, ref, sems[0].at[way, s, piece % 2], sems[1].at[way, s, piece % 2],
+            {"expert": right if way == 0 else left},
+        )
+
+    inside = lax.broadcasted_iota(jnp.int32, (rows, rows), 1) <= lax.broadcasted_iota(
+        jnp.int32, (rows, rows), 0
+    )
+    state = {}
+
+    def attend(blocks):
+        keys = jnp.concatenate([kv[b, 0] for b in blocks], axis=0)
+        vals = jnp.concatenate([kv[b, 1] for b in blocks], axis=0)
         for h in range(group):
-            scores[block, h] = lax.dot_general(
-                q_ref[:, h * HEAD_WIDTH : (h + 1) * HEAD_WIDTH],
-                kv[block, 0],
-                NT,
+            s_h = lax.dot_general(
+                q_ref[:, h * HEAD_WIDTH : (h + 1) * HEAD_WIDTH], keys, NT,
                 preferred_element_type=F32,
-            )
+            ) * HEAD_WIDTH ** (-0.5)
+            if h not in state:
+                s_h = jnp.where(inside, s_h, -jnp.inf)
+            else:
+                s_h = jnp.concatenate(
+                    [
+                        s_h[:, k * rows : (k + 1) * rows] + jnp.where(b < z, 0.0, -jnp.inf)
+                        for k, b in enumerate(blocks)
+                    ],
+                    axis=1,
+                )
+            top_h = jnp.max(s_h, axis=1, keepdims=True)
+            if h in state:
+                top_h = jnp.maximum(top_h, state[h][0])
+            e_h = jnp.exp(s_h - top_h)
+            sum_h = jnp.sum(e_h, axis=1, keepdims=True)
+            o_h = jnp.dot(e_h.astype(BF16), vals, preferred_element_type=F32)
+            if h in state:
+                shrink = jnp.exp(state[h][0] - top_h)
+                sum_h = sum_h + state[h][1] * shrink
+                o_h = o_h + state[h][2] * shrink
+            state[h] = (top_h, sum_h, o_h)
 
     for s in range(hops):
-        for way in range(2):
-            if s > 0:
-                kv_hop(way, s - 1).wait_recv()
-            go(kv_hop(way, s))
-        for way in range(2):
-            if s > 0:
-                w_hop(way, s - 1).wait_recv()
-            go(w_hop(way, s))
-        score(lax.rem(z + n_z - s, n_z))
-        if s > 0:
-            score(lax.rem(z + s, n_z))
+        for piece in range(4):
+            for way in range(2):
+                if s > 0:
+                    hop(way, s - 1, piece).wait_recv()
+                if s < hops - 1 or piece % 2 == way:
+                    go(hop(way, s, piece))
+        attend([z] if s == 0 else [lax.rem(z + n_z - s, n_z), lax.rem(z + s, n_z)])
     for way in range(2):
-        kv_hop(way, hops - 1).wait_recv()
-    score(lax.rem(z + hops, n_z))
+        hop(way, hops - 1, way).wait_recv()
+    attend([lax.rem(z + hops, n_z)])
+
+    turns = [0] + sorted(range(1, n_y), key=lambda d: min(d, n_y - d))
 
     def heads_copy(d, h):
         return remote(
@@ -153,22 +173,13 @@
             {"dp": lax.rem(y + d, n_y)},
         )
 
-    all_values = kv[:, 1].reshape(n_z * rows, HEAD_WIDTH)
-    shape = (rows, n_z * rows)
-    causal = lax.broadcasted_iota(jnp.int32, shape, 1) <= (
-        lax.broadcasted_iota(jnp.int32, shape, 0) + z * rows
-    )
     for h in range(group):
-        s_h = jnp.concatenate([scores[b, h] for b in range(n_z)], axis=1) * HEAD_WIDTH ** (-0.5)
-        s_h = jnp.where(causal, s_h, -jnp.inf)
-        e_h = jnp.exp(s_h - jnp.max(s_h, axis=1, keepdims=True))
-        a_h = (e_h * (1.0 / jnp.sum(e_h, axis=1, keepdims=True))).astype(BF16)
-        o_h = jnp.dot(a_h, all_values, preferred_element_type=F32)
+        o_h = state[h][2] * (1.0 / state[h][1])
         heads[y, h] = o_h.astype(BF16)
-        for d in range(1, n_y):
+        for d in turns[:0:-1]:
             go(heads_copy(d, h))
     for way in range(2):
-        w_hop(way, hops - 1).wait_recv()
+        hop(way, hops - 1, 2 + way).wait_recv()
 
     sibling = {"tensor": t + 1 - 2 * c}
     w_all = w[...].reshape(ycols, w.shape[2])
@@ -192,7 +203,6 @@
         for d in others[::-1]:
             go(head_cross(d, j))
 
-    turns = [0] + sorted(range(1, n_y), key=lambda d: min(d, n_y - d))
     for k, j in enumerate(turns):
         g = lax.rem(y + n_y - j, n_y)
         if j > 0:
@@ -325,7 +335,7 @@
     def share(p):
         if p > 0:
             slot_copy(p).wait_recv()
-        for d in others:
+        for d in others[::-1]:
             go(share_copy(p, d))
         go(pass_copy(p, 0))
 
@@ -458,19 +468,23 @@
         gate = jnp.where(expert == e, gates, 0.0)
         gate = jnp.sum(gate, axis=0, keepdims=True)
         pieces.append(jnp.where(table[pl.ds(e, 1), :] == slot, gate, 0.0))
-    comb = jnp.transpose(jnp.concatenate(pieces, axis=0))
-    high = comb.astype(BF16)
-    comb_hi[...] = high
-    comb_lo[...] = (comb - high.astype(F32)).astype(BF16)
+    combine = jnp.concatenate(pieces, axis=0)
     for q in range(units_half, n_units)[::-1]:
         reduce_recv(q)
-    for p in range(1, n_z):
-        return_copy(p).wait_recv()
-
-    back = zbuf[...]
-    mixture = jnp.dot(comb_hi[...], back, preferred_element_type=F32) + jnp.dot(
-        comb_lo[...], back, preferred_element_type=F32
-    )
+    mixture = jnp.zeros((rows, tcols), F32)
+    for first, last in [(0, units_half)] + [(q, q + 1) for q in range(units_half, n_units)[::-1]]:
+        for p in range(first * per_unit, last * per_unit):
+            if p > 0:
+                return_copy(p).wait_recv()
+        span = slice(first * urows, last * urows)
+        back = zbuf[span]
+        weights = combine[span]
+        high = weights.astype(BF16)
+        low = (weights - high.astype(F32)).astype(BF16)
+        for term in (high, low):
+            mixture = mixture + lax.dot_general(
+                term, back, (((0,), (0,)), ((), ())), preferred_element_type=F32
+            )
     mix[...] = mixture.astype(BF16).reshape(n_t, trows, tcols)
 
     def final_copy(d):
@@ -484,7 +498,7 @@
         final_copy(d).wait_recv()
     for i in range(n_t):
         span = slice(i * tcols, (i + 1) * tcols)
-        out_ref[:, span] = (mixed_ref[:, span] + fin[i].astype(F32)).astype(BF16)
+        out_ref[i] = (mixed_ref[:, span] + fin[i].astype(F32)).astype(BF16)
 
     for copy in sent:
         copy.wait_send()
@@ -519,7 +533,7 @@
 
     out = pl.pallas_call(
         functools.partial(block_kernel, n_y, n_z, n_t, slot_order(n_z)),
-        out_shape=jax.ShapeDtypeStruct((trows, width), BF16),
+        out_shape=jax.ShapeDtypeStruct((n_t, trows, tcols), BF16),
         in_specs=[hbm] * 11,
         out_specs=pl.BlockSpec(memory_space=pltpu.VMEM),
         scratch_shapes=[
@@ -532,7 +546,6 @@
             V((n_t, trows, 128), F32),
             V((n_z, 2, rows, HEAD_WIDTH), BF16),
             V((n_z, wcols, qcols), BF16),
-            V((n_z, qcols // HEAD_WIDTH, rows, rows), F32),
             V((n_y, group, rows, HEAD_WIDTH), BF16),
             V((2, n_y, n_x, trows, ycols), BF16),
             V((n_y, n_x, trows, ycols), BF16),
@@ -556,12 +569,10 @@
             V((n_units, n_x - 1, urows, tcols), BF16),
             V((n_z, CAP, tcols), BF16),
             V((n_z * CAP, tcols), BF16),
-            V((rows, n_z * CAP), BF16),
-            V((rows, n_z * CAP), BF16),
             V((n_t, trows, tcols), BF16),
             V((n_t, trows, tcols), BF16),
             dma((7,)), dma,
-            dma((2, hops)), dma((2, hops)), dma((2, hops)), dma((2, hops)),
+            dma((2, hops, 2)), dma((2, hops, 2)), dma((2, hops, 2)), dma((2, hops, 2)),
             dma((n_y - 1, group)), dma((n_y - 1, group)), dma((n_y,)), dma((n_y,)),
             dma((n_x - 1, n_y)), dma((n_x - 1, n_y)), dma((n_y - 1,)), dma((n_y - 1,)),
             dma((n_t - 1,)), dma((n_t - 1,)), dma((n_t - 1,)), dma((n_t - 1,)),
@@ -580,7 +591,7 @@
         router_weight.T, expert_ids[0].T,
         jnp.swapaxes(gate_weight, 1, 2)[0], jnp.swapaxes(up_weight, 1, 2)[0], down_weight[0],
     )
-    return out[None]
+    return jnp.swapaxes(out, 0, 1).reshape(1, trows, width)
 
 
 def solution(mesh):

time: 109 us -> 108 us (level)
    unnamed x1 -> x0, local copies, waits for them, and re-layouts: 1.54 us -> none
where the time goes in v6:
time: 108 us
  Pallas kernels  106 us (98%)
  local copies, waits for them, and re-layouts  1.6 us (1%)
    pallas_call x1, Pallas kernels, local(): pl.pallas_call(functools.partial(block_kernel, n_y, n_z, n_t, slot_order(...  106 us

profile of v6, /device:TPU:1, one launch (start us, length us, event | category | flops | bytes accessed | tf_op | source)
XLA Modules:
  0.0 108.1 jit_solution(17730185342079829207)
XLA Ops:
  0.0 106.5 %shard_map.109 = bf16[8,16,384]{2,1,0:T(8,128)(2,1)} custom-call(bf16[128,384]{1,0:T(8,128)(2,1)} %bitcast.23, bf16[128,128]{1,0:T(8,128)(2,1)} %bitcast.26, bf16[128,128]{1,0:T(8,128)(2,1)} %bitcast.27, bf16[96,384]{1,0:T(8,128)(2,1)} %bitcast.24, bf16[128,3072]{1,0:T(8,128)(2,1)} %bitcast.21, f32[1,3072]{1,0:T(1,128)} %bitcast.28, ...), custom_call_target="tpu_custom_call" | custom-call | tf_op jit(solution)/shard_map/pallas_call | solution.py:534
  106.5 0.9 copy.12
  107.4 0.7 reshape.3

commit v7 on v6

--- a/solution.py
+++ b/solution.py
@@ -102,9 +102,6 @@
     for i in range(n_x):
         span = pl.ds(i * xcols, xcols)
         loads.append(pltpu.make_async_copy(wd_ref.at[:, span], wd.at[i], wsem.at[2, i]))
-    for load in loads:
-        load.start()
-
     hops = n_z // 2
 
     def hop(way, s, piece):
@@ -160,6 +157,9 @@
                     hop(way, s - 1, piece).wait_recv()
                 if s < hops - 1 or piece % 2 == way:
                     go(hop(way, s, piece))
+        if s == 0:
+            for load in loads:
+                load.start()
         attend([z] if s == 0 else [lax.rem(z + n_z - s, n_z), lax.rem(z + s, n_z)])
     for way in range(2):
         hop(way, hops - 1, way).wait_recv()

time: 108 us -> 108 us (level)
  no operation moved by 1% of the time
where the time goes in v7:
time: 108 us
  Pallas kernels  107 us (99%)
  local copies, waits for them, and re-layouts  1.6 us (1%)
    pallas_call x1, Pallas kernels, local(): pl.pallas_call(functools.partial(block_kernel, n_y, n_z, n_t, slot_order(...  107 us

profile of v7, /device:TPU:1, one launch (start us, length us, event | category | flops | bytes accessed | tf_op | source)
XLA Modules:
  0.0 108.2 jit_solution(13357849595858786494)
XLA Ops:
  0.0 106.6 %shard_map.109 = bf16[8,16,384]{2,1,0:T(8,128)(2,1)} custom-call(bf16[128,384]{1,0:T(8,128)(2,1)} %bitcast.23, bf16[128,128]{1,0:T(8,128)(2,1)} %bitcast.26, bf16[128,128]{1,0:T(8,128)(2,1)} %bitcast.27, bf16[96,384]{1,0:T(8,128)(2,1)} %bitcast.24, bf16[128,3072]{1,0:T(8,128)(2,1)} %bitcast.21, f32[1,3072]{1,0:T(1,128)} %bitcast.28, ...), custom_call_target="tpu_custom_call" | custom-call | tf_op jit(solution)/shard_map/pallas_call | solution.py:534
  106.6 0.9 copy.12
  107.5 0.7 reshape.3
